TPU v7x, 32 devices: a whole 2x2x4 slice. The times are simulated.
32 devices in a mesh: replica: 4 (over x, core), shard: 8 (over z, y).
Axes of the slice: x: 2, y: 2, z: 4, core: 2. Of those that a mesh axis runs over, the one named last changes fastest.
Arguments:
- tokens: bfloat16 [8192, 1088], P(('replica', 'shard')), may hold values from -6 to 6
- slot: int32 [8192], P(('replica', 'shard')), may hold values from 0 to 2047, as said below
- lengths: int32 [4, 6], P('replica'), may hold values from 1 to 1024, 2048 in all within a row
- attn_in_weight: bfloat16 [1088, 3264], P('shard'), may hold values from -0.1875 to 0.1875
- attn_out_weight: bfloat16 [1088, 1088], P('shard'), may hold values from -2.5 to 2.5
- up_weight: bfloat16 [1088, 4352], P('shard'), may hold values from -0.1875 to 0.1875
- down_weight: bfloat16 [4352, 1088], P('shard'), may hold values from -0.09375 to 0.09375
- norm_gains: float32 [2, 1088], replicated, may hold values from 0.1 to 1.9
- layer_biases: float32 [6, 1088], replicated, may hold values from -0.6 to 0.6
- up_bias: float32 [4352], replicated, may hold values from -3 to 3
- cotangent: bfloat16 [8192, 1088], P(('replica', 'shard')), may hold values from -6 to 6
Outputs:
- mixed: bfloat16 [8192, 1088], P(('replica', 'shard'))
- tokens_grad: float32 [8192, 1088], P(('replica', 'shard'))
- attn_in_grad: float32 [1088, 3264], P('shard')
- attn_out_grad: float32 [1088, 1088], P('shard')
- up_grad: float32 [1088, 4352], P('shard')
- down_grad: float32 [4352, 1088], P('shard')
- gains_grad: float32 [2, 1088], P(None, 'shard')
- biases_grad: float32 [6, 1088], P(None, 'shard')
- up_bias_grad: float32 [4352], P('shard')
Inputs may be any that keep to these rules, and one draw needn't show every extreme that they name: `slot`: within each group's rows (blocks of 2048 rows in order), every place 0 to 2047 occurs exactly once. Each row of lengths sums to 2048; its largest entry is 1024.
All inputs are finite; a program needn't handle non-finite values.
Results may differ from a plain program's by a relative error of at most 0.02.
Values may be sent and summed in bfloat16 or wider, within the bound.
No kernel may reach another device: no remote copies, remote signals or barrier semaphores. Data moves between devices by JAX's collectives and lax.ppermute only.
A program may use at most 256 MiB of HBM per device.

v0:
```python
import jax
import jax.numpy as jnp
from jax import lax
from jax.sharding import PartitionSpec as P

HEADS = 17
HEAD = 64


def norm_apply(values, gain_row, bias_row):
    centre = values - jnp.mean(values, axis=-1, keepdims=True)
    spread = jnp.mean(centre * centre, axis=-1, keepdims=True)
    return centre * lax.rsqrt(spread + 1e-05) * gain_row + bias_row


def gelu_tanh(values):
    return jax.nn.gelu(values, approximate=True)


def contract_rows(left, right):
    return lax.dot_general(
        left, right, (((0,), (0,)), ((), ())), preferred_element_type=jnp.float32
    )


def contract_cols(left, right):
    return lax.dot_general(
        left, right, (((1,), (1,)), ((), ())), preferred_element_type=jnp.float32
    )


def by_blocks(step_fn, state_now, shard_piece):
    row_count = shard_piece.shape[0]
    block_rows = 512
    block_count = row_count // block_rows
    stacked = shard_piece.reshape((block_count, block_rows) + shard_piece.shape[1:])
    offsets = jnp.arange(block_count, dtype=jnp.int32) * block_rows

    def advance(state_inner, inputs_now):
        return (step_fn(state_inner, inputs_now[0], inputs_now[1]), None)

    state_out, unused = lax.scan(advance, state_now, (stacked, offsets))
    return state_out


def owner_blocks(gradient, owners, split_dim):
    if split_dim == 0:
        return gradient.reshape(owners, -1)
    leading = gradient.shape[0]
    return gradient.reshape(leading, owners, -1).transpose(1, 0, 2).reshape(owners, -1)


def unpack_owned(owned_flat, full_grads, split_dims, member_widths, owners):
    results = []
    offset = 0
    for member, dim_now, width_now in zip(full_grads, split_dims, member_widths):
        segment = owned_flat[offset : offset + width_now]
        offset = offset + width_now
        if dim_now == 0:
            results.append(segment.reshape((member.shape[0] // owners,) + member.shape[1:]))
        else:
            results.append(segment.reshape(member.shape[0], member.shape[1] // owners))
    return tuple(results)


def shards(
    tokens,
    slot,
    lengths,
    attn_in_weight,
    attn_out_weight,
    up_weight,
    down_weight,
    norm_gains,
    layer_biases,
    up_bias,
    cotangent,
):
    tok_rows = tokens.shape[0]
    feat_count = tokens.shape[1]
    head_count = HEADS
    head_size = HEAD
    ends = jnp.cumsum(lengths[0])
    docs = jnp.sum((slot[:, None] >= ends[None, :]).astype(jnp.int32), axis=1)
    all_places = lax.all_gather(jnp.stack([slot, docs]), "shard", axis=1, tiled=True)
    inputs_f = tokens.astype(jnp.float32)
    h_first_f, first_norm_back = jax.vjp(norm_apply, inputs_f, norm_gains[0], layer_biases[0])
    h_first = h_first_f.astype(jnp.bfloat16)
    w_in, w_out = (
        lax.all_gather(attn_in_weight, "shard", axis=0, tiled=True),
        lax.all_gather(attn_out_weight, "shard", axis=0, tiled=True),
    )
    projected = jnp.dot(h_first, w_in, preferred_element_type=jnp.float32)
    query = (projected[:, :feat_count] + layer_biases[1]).astype(jnp.bfloat16)
    keys = projected[:, feat_count : 2 * feat_count].astype(jnp.bfloat16)
    values = (projected[:, 2 * feat_count :] + layer_biases[2]).astype(jnp.bfloat16)
    key_value = jnp.concatenate([keys, values], axis=1)
    query_heads = query.reshape(tok_rows, head_count, head_size)

    def masked_scores(pair_part, first_row):
        part_rows = pair_part.shape[0]
        key_heads = pair_part[:, :feat_count].reshape(part_rows, head_count, head_size)
        value_heads = pair_part[:, feat_count:].reshape(part_rows, head_count, head_size)
        places = lax.dynamic_slice_in_dim(all_places, first_row, part_rows, 1)
        slot_part = places[0]
        doc_part = places[1]
        scores = (
            jnp.einsum("thd,shd->hts", query_heads, key_heads, preferred_element_type=jnp.float32)
            * 0.125
        )
        allowed = (doc_part[None, :] == docs[:, None]) & (slot_part[None, :] <= slot[:, None])
        return (jnp.where(allowed[None], scores, -1e30), allowed, key_heads, value_heads)

    def forward_step(state_now, pair_part, first_row):
        accumulated = state_now[:, :, :head_size]
        running_max = state_now[:, :, head_size].T
        denominator = state_now[:, :, head_size + 1].T
        scores, allowed, key_heads, value_heads = masked_scores(pair_part, first_row)
        new_max = jnp.maximum(running_max, jnp.max(scores, axis=-1))
        weights = jnp.where(allowed[None], jnp.exp(scores - new_max[..., None]), 0.0)
        rescale = jnp.exp(running_max - new_max)
        accumulated = accumulated * rescale.T[:, :, None] + jnp.einsum(
            "hts,shd->thd",
            weights.astype(jnp.bfloat16),
            value_heads,
            preferred_element_type=jnp.float32,
        )
        denominator = denominator * rescale + jnp.sum(weights, axis=-1)
        return jnp.concatenate(
            [accumulated, new_max.T[:, :, None], denominator.T[:, :, None]], axis=-1
        )

    start_state = jnp.concatenate(
        [
            jnp.zeros((tok_rows, head_count, head_size), jnp.float32),
            jnp.full((tok_rows, head_count, 1), -1e30, jnp.float32),
            jnp.zeros((tok_rows, head_count, 1), jnp.float32),
        ],
        axis=-1,
    )
    final_state = by_blocks(
        forward_step, start_state, lax.all_gather(key_value, "shard", axis=0, tiled=True)
    )
    accumulated = final_state[:, :, :head_size]
    running_max = final_state[:, :, head_size].T
    denominator = final_state[:, :, head_size + 1].T
    attended_f = accumulated / denominator.T[:, :, None]
    log_total = running_max + jnp.log(denominator)
    attended = attended_f.reshape(tok_rows, feat_count).astype(jnp.bfloat16)
    branch = jnp.dot(attended, w_out, preferred_element_type=jnp.float32) + layer_biases[3]
    middle = inputs_f + branch
    h_second_f, second_norm_back = jax.vjp(norm_apply, middle, norm_gains[1], layer_biases[4])
    h_second = h_second_f.astype(jnp.bfloat16)
    w_up, w_down = (
        lax.all_gather(up_weight, "shard", axis=0, tiled=True),
        lax.all_gather(down_weight, "shard", axis=0, tiled=True),
    )
    pre = jnp.dot(h_second, w_up, preferred_element_type=jnp.float32) + up_bias
    act_f, gelu_back = jax.vjp(gelu_tanh, pre)
    act = act_f.astype(jnp.bfloat16)
    mixed = (
        middle + jnp.dot(act, w_down, preferred_element_type=jnp.float32) + layer_biases[5]
    ).astype(jnp.bfloat16)
    w_in, w_out = (
        lax.all_gather(attn_in_weight, "shard", axis=0, tiled=True),
        lax.all_gather(attn_out_weight, "shard", axis=0, tiled=True),
    )
    w_up, w_down = (
        lax.all_gather(up_weight, "shard", axis=0, tiled=True),
        lax.all_gather(down_weight, "shard", axis=0, tiled=True),
    )
    grad_out = cotangent.astype(jnp.float32)
    down_grad = contract_rows(act, cotangent)
    down_bias_grad = jnp.sum(grad_out, axis=0)
    act_grad = contract_cols(cotangent, w_down)
    pre_grad = gelu_back(act_grad)[0].astype(jnp.bfloat16)
    up_grad = contract_rows(h_second, pre_grad)
    up_bias_grad = jnp.sum(pre_grad.astype(jnp.float32), axis=0)
    h_second_grad = contract_cols(pre_grad, w_up)
    middle_norm_grad, gain_two_grad, bias_two_grad = second_norm_back(h_second_grad)
    middle_grad = grad_out + middle_norm_grad
    branch_grad = middle_grad.astype(jnp.bfloat16)
    out_grad = contract_rows(attended, branch_grad)
    out_bias_grad = jnp.sum(branch_grad.astype(jnp.float32), axis=0)
    attended_grad = contract_cols(branch_grad, w_out).astype(jnp.bfloat16)
    attended_heads = attended_grad.reshape(tok_rows, head_count, head_size)
    delta = jnp.sum(attended_heads.astype(jnp.float32) * attended_f, axis=-1).T
    query_rows = tok_rows // 2

    def backward_step(state_now, pair_part, first_row):
        part_rows = pair_part.shape[0]
        scores, allowed, key_heads, value_heads = masked_scores(pair_part, first_row)
        prob = jnp.where(allowed[None], jnp.exp(scores - log_total[..., None]), 0.0)
        prob_low = prob.astype(jnp.bfloat16)
        prob_grad = jnp.einsum(
            "thd,shd->hts", attended_heads, value_heads, preferred_element_type=jnp.float32
        )
        score_grad = (prob * (prob_grad - delta[..., None])).astype(jnp.bfloat16)
        query_step = (
            jnp.einsum("hts,shd->thd", score_grad, key_heads, preferred_element_type=jnp.float32)
            * 0.125
        )
        key_grad = (
            jnp.einsum("hts,thd->shd", score_grad, query_heads, preferred_element_type=jnp.float32)
            * 0.125
        )
        value_grad = jnp.einsum(
            "hts,thd->shd", prob_low, attended_heads, preferred_element_type=jnp.float32
        )
        new_rows = jnp.concatenate(
            [key_grad.reshape(part_rows, feat_count), value_grad.reshape(part_rows, feat_count)],
            axis=1,
        )
        query_part = state_now[:query_rows] + query_step.reshape(query_rows, 2 * feat_count)
        state_now = lax.dynamic_update_slice_in_dim(state_now, query_part, 0, 0)
        row_at = query_rows + first_row
        previous = lax.dynamic_slice_in_dim(state_now, row_at, part_rows, 0)
        return lax.dynamic_update_slice_in_dim(state_now, previous + new_rows, row_at, 0)

    group_rows = tok_rows * lax.axis_size("shard")
    back_state = jnp.zeros((query_rows + group_rows, 2 * feat_count), jnp.float32)
    back_final = by_blocks(
        backward_step, back_state, lax.all_gather(key_value, "shard", axis=0, tiled=True)
    )
    query_grad = back_final[:query_rows].reshape(tok_rows, feat_count)
    pair_grad = back_final[query_rows:]
    own_pairs = lax.psum_scatter(
        pair_grad.astype(jnp.bfloat16), "shard", scatter_dimension=0, tiled=True
    )
    query_low = query_grad.astype(jnp.bfloat16)
    proj_grad = jnp.concatenate([query_low, own_pairs], axis=1)
    in_grad = contract_rows(h_first, proj_grad)
    query_bias_grad = jnp.sum(query_low.astype(jnp.float32), axis=0)
    value_bias_grad = jnp.sum(own_pairs[:, feat_count:].astype(jnp.float32), axis=0)
    h_first_grad = contract_cols(proj_grad, w_in)
    input_norm_grad, gain_one_grad, bias_one_grad = first_norm_back(h_first_grad)
    tokens_grad = middle_grad + input_norm_grad
    gains_grad = jnp.stack([gain_one_grad, gain_two_grad])
    biases_grad = jnp.stack(
        [
            bias_one_grad,
            query_bias_grad,
            value_bias_grad,
            out_bias_grad,
            bias_two_grad,
            down_bias_grad,
        ]
    )
    full_grads = (in_grad, out_grad, up_grad, down_grad, gains_grad, biases_grad, up_bias_grad)
    split_dims = (0, 0, 0, 0, 1, 1, 0)
    owners = lax.axis_size("shard")
    members = [
        owner_blocks(member, owners, dim_now) for member, dim_now in zip(full_grads, split_dims)
    ]
    member_widths = [member.shape[1] for member in members]
    packed = jnp.concatenate(members, axis=1)
    owned = lax.psum_scatter(
        packed.reshape(-1).astype(jnp.bfloat16), "shard", scatter_dimension=0, tiled=True
    )
    summed_piece = lax.psum_scatter(owned, "replica", scatter_dimension=0, tiled=True).astype(
        jnp.float32
    )
    owned_flat = lax.all_gather(
        summed_piece.astype(jnp.bfloat16), "replica", axis=0, tiled=True
    ).astype(summed_piece.dtype)
    summed = unpack_owned(owned_flat, full_grads, split_dims, member_widths, owners)
    return (
        mixed,
        tokens_grad,
        summed[0],
        summed[1],
        summed[2],
        summed[3],
        summed[4],
        summed[5],
        summed[6],
    )


def solution(mesh):
    in_specs = (
        P(("replica", "shard"), None),
        P(("replica", "shard")),
        P("replica", None),
        P("shard", None),
        P("shard", None),
        P("shard", None),
        P("shard", None),
        P(),
        P(),
        P(),
        P(("replica", "shard"), None),
    )
    out_specs = (
        P(("replica", "shard"), None),
        P(("replica", "shard"), None),
        P("shard", None),
        P("shard", None),
        P("shard", None),
        P("shard", None),
        P(None, "shard"),
        P(None, "shard"),
        P("shard"),
    )
    return jax.shard_map(shards, mesh=mesh, in_specs=in_specs, out_specs=out_specs, check_vma=False)
```

profile of v0, /device:TPU:0, one launch (start us, length us, event | category | flops | bytes accessed | tf_op | source)
XLA Modules:
  0.0 2300.7 jit_solution(10650875829050847536)
XLA Ops:
  11.0 112.8 %all-gather.6.cloned.1.call-done = bf16[1088,3264]{1,0:T(8,128)(2,1)} async-done(((bf16[136,3264]{1,0:T(8,128)(2,1)}), bf16[1088,3264]{1,0:T(8,128)(2,1)}) %all-gather.6.cloned.1.call-update) | async-done | bytes 7102480 | tf_op jit(solution)/shard_map/all_gather | solution.py:90
  133.5 26.7 %all_gather.26 = s32[2,2048]{1,0:T(2,128)S(1)} all-gather(s32[2,256]{1,0:T(2,128)S(1)} %pad_add_fusion), channel_id=1, replica_groups=mesh['replica'=4,'shard'=8] {'shard'}, dimensions={1}, use_global_device_ids=true | all-gather | bytes 18432 | tf_op jit(solution)/shard_map/all_gather | solution.py:85
  160.4 109.2 %all-gather.14.cloned.1.call-done = bf16[4352,1088]{1,0:T(8,128)(2,1)} async-done(((bf16[544,1088]{1,0:T(8,128)(2,1)}), bf16[4352,1088]{1,0:T(8,128)(2,1)}) %all-gather.14.cloned.1.call-update) | async-done | bytes 9469968 | tf_op jit(solution)/shard_map/all_gather | solution.py:156
  280.4 121.8 %all-gather.8.cloned.1.call-done = bf16[2048,2176]{0,1:T(8,128)(2,1)} async-done(((bf16[256,2176]{0,1:T(8,128)(2,1)}), bf16[2048,2176]{0,1:T(8,128)(2,1)}) %all-gather.8.cloned.1.call-update) | async-done | bytes 8912912 | tf_op jit(solution)/shard_map/all_gather | solution.py:142
  410.3 56.8 %while.22 = (s32[]{:T(128)}, f32[256,17,66]{0,2,1:T(8,128)S(1)}, s32[4]{0:T(128)S(1)}, s32[2,2048]{1,0:T(2,128)S(1)}, s32[256]{0:T(256)S(1)}, /*index=5*/s32[256...) while((s32[]{:T(128)}, f32[256,17,66]{0,2,1:T(8,128)S(1)}, ...), condition=%wide.region_7.8_spmd, body=%wide.region_4.7_spmd.sunk | while | flops 600930048 | bytes 46130368 | solution.py:42
  475.0 120.1 %all-gather.12.cloned.1.call-done = bf16[1088,4352]{1,0:T(8,128)(2,1)} async-done(((bf16[136,4352]{1,0:T(8,128)(2,1)}), bf16[1088,4352]{1,0:T(8,128)(2,1)}) %all-gather.12.cloned.1.call-update) | async-done | bytes 9469968 | tf_op jit(solution)/shard_map/all_gather | solution.py:155
  595.1 12.1 fusion.69
  622.4 250.5 %while.23 = (s32[]{:T(128)}, f32[2176,2176]{1,0:T(8,128)}, bf16[4,512,2176]{1,2,0:T(8,128)(2,1)}, s32[4]{0:T(128)S(1)}, s32[2,2048]{1,0:T(2,128)S(1)}, /*index=5...) while((s32[]{:T(128)}, f32[2176,2176]{1,0:T(8,128)}, ...), condition=%wide.region_14.15_spmd, body=%wide.region_13.14_spmd.sunk | while | flops 1456537600 | bytes 124126584 | solution.py:42
  673.2 12.2 dynamic_update_slice.16
  735.9 12.2 dynamic_update_slice.16
  798.5 12.2 dynamic_update_slice.16
  861.1 11.7 dynamic_update_slice.16
  912.5 11.8 reshape.371
  933.0 14.0 copy.79
  947.0 19.7 reshape.401
  966.8 11.5 reshape.372
  979.0 67.1 %reduce-scatter.2.cloned.1.call-done = bf16[256,2176]{1,0:T(8,128)(2,1)} async-done(((bf16[2048,2176]{1,0:T(8,128)(2,1)}), bf16[256,2176]{1,0:T(8,128)(2,1)}) %reduce-scatter.2.cloned.1.call-update) | async-done | bytes 1114128 | tf_op jit(solution)/shard_map/reduce_scatter | solution.py:227
  1057.6 14.3 reshape.397
  1071.9 13.5 reshape.369
  1114.7 150.6 %convert_element_type.107 = bf16[14217984]{0:T(1024)(128)(2,1)} reshape(bf16[8,1777248]{1,0:T(8,128)(2,1)} %dynamic-update-slice.7) | data formatting | bytes 56871936 | tf_op jit(solution)/shard_map/convert_element_type | solution.py:258
  1267.2 830.5 %all-reduce.9.cloned.1.call-done = bf16[14217984]{0:T(1024)(128)(2,1)} async-done(((bf16[14217984]{0:T(1024)(128)(2,1)}), bf16[14217984]{0:T(1024)(128)(2,1)}) %all-reduce.9.cloned.1.call-update) | async-done | bytes 28435984
  2104.9 72.0 %all-reduce.11.cloned.1.call-done = bf16[1777248]{0:T(1024)(128)(2,1)} async-done(((bf16[1777248]{0:T(1024)(128)(2,1)}), bf16[1777248]{0:T(1024)(128)(2,1)}) %all-reduce.11.cloned.1.call-update) | async-done | bytes 3554512
  2181.4 14.9 dynamic-update-slice
  2208.2 63.6 %all-reduce.7.cloned.1.call-done = bf16[1777248]{0:T(1024)(128)(2,1)} async-done(((bf16[1777248]{0:T(1024)(128)(2,1)}), bf16[1777248]{0:T(1024)(128)(2,1)}) %all-reduce.7.cloned.1.call-update) | async-done | bytes 3554512
  (381 shorter events, 428.3 us)
Async XLA Ops:
  7.2 116.5 %all-gather.6.cloned.1.call-start = ((), (), s32[]{:S(2)}) async-start(), calls=%async_computation.1 | async-start | bytes 8146944 | tf_op jit(solution)/shard_map/all_gather | solution.py:90
  7.9 261.6 %all-gather.14.cloned.1.call-start = ((), (), s32[]{:S(2)}) async-start(), calls=%async_computation.5 | async-start | bytes 11280384 | tf_op jit(solution)/shard_map/all_gather | solution.py:156
  8.7 393.5 %all-gather.8.cloned.1.call-start = ((), (), s32[]{:S(2)}) async-start(), calls=%async_computation.2 | async-start | bytes 10027008 | tf_op jit(solution)/shard_map/all_gather | solution.py:142
  10.5 119.9 %copy-start.22 = (f32[1088]{0:T(1024)}, f32[1088]{0:T(1024)S(1)}, u32[]{:S(2)}) copy-start(f32[1088]{0:T(1024)S(1)} %get-tuple-element.350) | copy-start | bytes 13060
  10.5 119.9 %copy-start.27 = (f32[1088]{0:T(1024)}, f32[1088]{0:T(1024)S(1)}, u32[]{:S(2)}) copy-start(f32[1088]{0:T(1024)S(1)} %get-tuple-element.277) | copy-start | bytes 13060
  10.5 584.6 %copy-start.29 = (f32[1088]{0:T(1024)}, f32[1088]{0:T(1024)S(1)}, u32[]{:S(2)}) copy-start(f32[1088]{0:T(1024)S(1)} %get-tuple-element.273) | copy-start | bytes 13060
  10.5 600.2 %copy-start.25 = (f32[1088]{0:T(1024)}, f32[1088]{0:T(1024)S(1)}, u32[]{:S(2)}) copy-start(f32[1088]{0:T(1024)S(1)} %get-tuple-element.351) | copy-start | bytes 13060
  10.7 119.7 %copy-start.31 = (f32[256]{0:T(256)}, f32[256]{0:T(256)S(1)}, u32[]{:S(2)}) copy-start(f32[256]{0:T(256)S(1)} %broadcast_multiply_fusion.1) | copy-start | bytes 3076
  10.9 119.5 %copy-start.43 = (f32[256]{0:T(256)}, f32[256]{0:T(256)S(1)}, u32[]{:S(2)}) copy-start(f32[256]{0:T(256)S(1)} %fusion.50) | copy-start | bytes 3076
  10.9 119.5 %copy-start.35 = (f32[256]{0:T(256)}, f32[256]{0:T(256)S(1)}, u32[]{:S(2)}) copy-start(f32[256]{0:T(256)S(1)} %fusion.60) | copy-start | bytes 3076
  130.9 138.6 %copy-start.16 = (bf16[256,1088]{0,1:T(8,128)(2,1)S(1)}, bf16[256,1088]{0,1:T(8,128)(2,1)}, u32[]{:S(2)}) copy-start(bf16[256,1088]{0,1:T(8,128)(2,1)} %param.25) | copy-start | bytes 1671172
  132.0 337.3 %all-gather.10.cloned.1.call-start = ((), (), s32[]{:S(2)}) async-start(), calls=%async_computation.3 | async-start | bytes 2820096 | tf_op jit(solution)/shard_map/all_gather | solution.py:91
  132.6 462.5 %all-gather.12.cloned.1.call-start = ((), (), s32[]{:S(2)}) async-start(), calls=%async_computation.4 | async-start | bytes 10653696 | tf_op jit(solution)/shard_map/all_gather | solution.py:155
  133.2 912.9 %reduce-scatter.2.cloned.1.call-start = ((), (), s32[]{:S(2)}) async-start(), calls=%async_computation.6 | async-start | bytes 10027008 | tf_op jit(solution)/shard_map/reduce_scatter | solution.py:227
  472.5 138.3 %copy-start.33 = (f32[256]{0:T(256)}, f32[256]{0:T(256)S(1)}, u32[]{:S(2)}) copy-start(f32[256]{0:T(256)S(1)} %broadcast_multiply_fusion) | copy-start | bytes 3076
  473.6 137.2 %copy-start.38 = (f32[256]{0:T(256)}, f32[256]{0:T(256)S(1)}, u32[]{:S(2)}) copy-start(f32[256]{0:T(256)S(1)} %fusion.61) | copy-start | bytes 3076
  891.6 1206.1 %all-reduce.9.cloned.1.call-start = ((), (), s32[]{:S(2)}) async-start(), calls=%async_computation.8 | async-start | bytes 56872960
  966.7 79.4 %copy-start.4 = (bf16[256,1088]{0,1:T(8,128)(2,1)S(1)}, bf16[256,1088]{0,1:T(8,128)(2,1)}, u32[]{:S(2)}) copy-start(bf16[256,1088]{0,1:T(8,128)(2,1)} %param.15) | copy-start | bytes 1671172
  966.8 79.4 %copy-start.23 = (f32[1088]{0:T(1024)S(1)}, f32[1088]{0:T(1024)}, u32[]{:S(2)}) copy-start(f32[1088]{0:T(1024)} %copy-done.22) | copy-start | bytes 13060
  966.8 79.4 %copy-start.32 = (f32[256]{0:T(256)S(1)}, f32[256]{0:T(256)}, u32[]{:S(2)}) copy-start(f32[256]{0:T(256)} %copy-done.31) | copy-start | bytes 3076
  979.0 73.8 %copy-start.28 = (f32[1088]{0:T(1024)S(1)}, f32[1088]{0:T(1024)}, u32[]{:S(2)}) copy-start(f32[1088]{0:T(1024)} %copy-done.27) | copy-start | bytes 13060
  979.0 73.8 %copy-start.36 = (f32[256]{0:T(256)S(1)}, f32[256]{0:T(256)}, u32[]{:S(2)}) copy-start(f32[256]{0:T(256)} %copy-done.35) | copy-start | bytes 3076
  1265.4 911.5 %all-reduce.11.cloned.1.call-start = ((), (), s32[]{:S(2)}) async-start(), calls=%async_computation.9 | async-start | bytes 7110656
  2102.4 169.4 %all-reduce.7.cloned.1.call-start = ((), (), s32[]{:S(2)}) async-start(), calls=%async_computation.7 | async-start | bytes 7110656
  (58 other events, 411.9 us)
Sparse Core Ops, SparseCore 0:
  10.2 113.4 all-gather.5
  125.9 143.5 all-gather.13
  272.2 129.9 all-gather.7
  404.2 51.7 all-gather.9
  458.0 137.0 all-gather.11
  891.8 154.3 reduce-scatter.1
  1265.5 832.1 all-reduce.8
  2102.5 74.3 all-reduce.10
  2196.4 75.2 all-reduce.6
where the time goes:
time: 2310 us; the launch traced here: 2300 us
  waiting for transfers between devices  1500 us (65%)
  local copies, waits for them, and re-layouts  472 us (20%)
  matrix products  192 us (8%)
  other arithmetic  71.3 us (3%)
  blocking collectives  26.7 us (1%)
    unnamed x12, waiting for transfers between devices  969 us
    convert_element_type x1, local copies, waits for them, and re-layouts, shards(): packed.reshape(-1).astype(jnp.bfloat16)  151 us
    all_gather x1, waiting for transfers between devices, shards(): lax.all_gather(key_value, 'shard', axis=0, tiled=True)  122 us
    all_gather x1, waiting for transfers between devices, shards(): lax.all_gather(up_weight, 'shard', axis=0, tiled=True)  120 us
    all_gather x1, waiting for transfers between devices, shards(): lax.all_gather(attn_in_weight, 'shard', axis=0, tiled=True)  113 us
    all_gather x1, waiting for transfers between devices, shards(): lax.all_gather(down_weight, 'shard', axis=0, tiled=True)  109 us
    unnamed x132, local copies, waits for them, and re-layouts  94 us
    reduce_scatter x1, waiting for transfers between devices, shards(): lax.psum_scatter(pair_grad.astype(jnp.bfloat16), 'shard', scatter_dimensi...  67.1 us
  transfers between devices with their start and end apart: 9, of which 8 were waited for; matrix products, arithmetic and copies ran while one was open for 8% of the time, Pallas kernels for 0%

commit v1 on v0

v1 whole, which is shorter than its diff:
```python
import functools

import jax
import jax.numpy as jnp
from jax import lax
from jax.experimental import pallas as pl
from jax.experimental.pallas import tpu as pltpu
from jax.sharding import Mesh, PartitionSpec as P

HEAD = 64
BF = jnp.bfloat16
F32 = jnp.float32
REP = ("x", "core")
SHARD = ("z", "y")
NEG = -1e30


def dot(left, right):
    return jnp.dot(left, right, preferred_element_type=F32)


def dot_nt(left, right):
    return lax.dot_general(left, right, (((1,), (1,)), ((), ())), preferred_element_type=F32)


def dot_tn(left, right):
    return lax.dot_general(left, right, (((0,), (0,)), ((), ())), preferred_element_type=F32)


def iota(shape, dim):
    return lax.broadcasted_iota(jnp.int32, shape, dim)


def doc_starts(places, ends_ref):
    starts = jnp.zeros_like(places)
    for n in range(ends_ref.shape[0]):
        starts = jnp.where(places >= ends_ref[n], ends_ref[n], starts)
    return starts


def first_block(block, tile, ends_ref):
    row = block * tile
    start = jnp.int32(0)
    for n in range(ends_ref.shape[0]):
        start = jnp.where(row >= ends_ref[n], ends_ref[n], start)
    return lax.div(start, jnp.int32(tile))


def rows(block, tile):
    return pl.ds(pl.multiple_of(block * tile, tile), tile)


def only_head(values, head):
    lanes = iota(values.shape, 1)
    keep = (lanes < HEAD) if head == 0 else (lanes >= HEAD)
    return jnp.where(keep, values, jnp.zeros_like(values))


def forward_kernel(
    ends_ref, me_ref, h_ref, w_ref, b_ref, srow_ref, scol_ref, own_ref,
    sp_ref, kt_ref, o_ref, of_ref, lse_ref, q16_ref, o16_ref, lse16_ref,
    p_scr, vt_scr, ob_scr,
):
    total = h_ref.shape[0]
    tile = own_ref.shape[1]
    blocks = total // tile

    @pl.loop(0, blocks)
    def _(b):
        r = rows(b, tile)
        p_scr[r, :] = (dot(h_ref[r, :], w_ref[...]) + b_ref[...]).astype(BF)

    @pl.loop(0, blocks)
    def _(b):
        r = rows(b, tile)
        place = iota((tile, total), 0) + b * tile
        pick = jnp.where(srow_ref[...] == place, 1.0, 0.0).astype(BF)
        sorted_f = dot(pick, p_scr[:, :512])
        sp_ref[r, :] = sorted_f.astype(BF)
        kt_ref[b] = sorted_f[:, 128:256].T.astype(BF)
        vt_scr[b, :128, :] = sorted_f[:, 256:384].T.astype(BF)
        vt_scr[b, 128:, :] = sorted_f[:, 384:512].T.astype(BF)

    q16 = p_scr[rows(me_ref[0], tile), 512:640]
    q16_ref[...] = q16

    @pl.loop(0, blocks)
    def _(qb):
        q = sp_ref[rows(qb, tile), 0:128]
        qs = [only_head(q, 0), only_head(q, 1)]
        qpos = iota((1, tile), 1) + qb * tile
        qstart = doc_starts(qpos, ends_ref)
        low = first_block(qb, tile, ends_ref)

        def step(n, state):
            kb = qb - n
            k = sp_ref[rows(kb, tile), 128:256]
            kpos = iota((tile, tile), 0) + kb * tile
            ok = (kpos <= qpos) & (kpos >= qstart)
            new = []
            for head in range(2):
                m, l, acc = state[head]
                s = jnp.where(ok, dot_nt(k, qs[head]) * 0.125, NEG)
                mn = jnp.maximum(m, jnp.max(s, axis=0, keepdims=True))
                p = jnp.exp(s - mn)
                a = jnp.exp(m - mn)
                l = l * a + jnp.sum(p, axis=0, keepdims=True)
                vt = vt_scr[kb, head * HEAD:(head + 1) * HEAD, :]
                acc = acc * a + dot(vt, p.astype(BF))
                new.append((mn, l, acc))
            return tuple(new)

        start = (jnp.full((1, tile), NEG, F32), jnp.zeros((1, tile), F32), jnp.zeros((HEAD, tile), F32))
        state = lax.fori_loop(0, qb - low + 1, step, (start, start))
        out = jnp.concatenate([state[0][2] / state[0][1], state[1][2] / state[1][1]], axis=0).T
        of_ref[rows(qb, tile), :] = out
        ob_scr[rows(qb, tile), :] = out.astype(BF)
        lse_ref[qb] = jnp.concatenate([s[0] + jnp.log(s[1]) for s in state], axis=0)

    own = own_ref[...]
    own_start = doc_starts(own, ends_ref)

    def step16(kb, state):
        m, l, acc = state
        kv = sp_ref[rows(kb, tile), 384:512]
        kpos = iota((tile, tile), 0) + kb * tile
        ok = (kpos <= own) & (kpos >= own_start)
        s = jnp.where(ok, dot_nt(kv, q16) * 0.125, NEG)
        mn = jnp.maximum(m, jnp.max(s, axis=0, keepdims=True))
        p = jnp.where(ok, jnp.exp(s - mn), 0.0)
        a = jnp.exp(m - mn)
        l = l * a + jnp.sum(p, axis=0, keepdims=True)
        acc = acc * a + dot(vt_scr[kb, 192:256, :], p.astype(BF))
        return mn, l, acc

    start = (jnp.full((1, tile), NEG, F32), jnp.zeros((1, tile), F32), jnp.zeros((HEAD, tile), F32))
    m, l, acc = lax.fori_loop(0, blocks, step16, start)
    o16_ref[...] = jnp.concatenate([jnp.zeros_like(acc), acc / l], axis=0).T
    lse16_ref[...] = m + jnp.log(l)

    @pl.loop(0, blocks)
    def _(b):
        r = rows(b, tile)
        pick = jnp.where(scol_ref[r, :] == iota((tile, total), 1), 1.0, 0.0).astype(BF)
        o_ref[r, :] = dot(pick, ob_scr[...]).astype(BF)


def backward_kernel(
    ends_ref, srow_ref, scol_ref, own_ref, sp_ref, kt_ref, of_ref, lse_ref,
    do_ref, q16_ref, do16_ref, o16_ref, lse16_ref,
    dp_ref, dq16_ref,
    dos_scr, acc_scr, acc16_scr, dps_scr,
):
    total = sp_ref.shape[0]
    tile = own_ref.shape[1]
    blocks = total // tile

    @pl.loop(0, blocks)
    def _(b):
        r = rows(b, tile)
        place = iota((tile, total), 0) + b * tile
        pick = jnp.where(srow_ref[...] == place, 1.0, 0.0).astype(BF)
        dos_scr[r, :] = dot(pick, do_ref[...]).astype(BF)
        acc_scr[r, :] = jnp.zeros((tile, 256), F32)

    @pl.loop(0, blocks)
    def _(qb):
        qr = rows(qb, tile)
        q = sp_ref[qr, 0:128]
        do = dos_scr[qr, :]
        qs = [only_head(q, 0), only_head(q, 1)]
        ds_ = [only_head(do, 0), only_head(do, 1)]
        q_two = jnp.concatenate(qs, axis=0)
        do_two = jnp.concatenate(ds_, axis=0)
        prod = (do.astype(F32) * of_ref[qr, :]).T
        delta = [jnp.sum(prod[:HEAD], axis=0, keepdims=True), jnp.sum(prod[HEAD:], axis=0, keepdims=True)]
        lse = lse_ref[qb]
        qpos = iota((1, tile), 1) + qb * tile
        qstart = doc_starts(qpos, ends_ref)
        low = first_block(qb, tile, ends_ref)

        def step(kb, dqt):
            kr = rows(kb, tile)
            k = sp_ref[kr, 128:256]
            v = sp_ref[kr, 256:384]
            kpos = iota((tile, tile), 0) + kb * tile
            ok = (kpos <= qpos) & (kpos >= qstart)
            ps, dss, new = [], [], []
            for head in range(2):
                s = dot_nt(k, qs[head]) * 0.125 - lse[head:head + 1]
                p = jnp.where(ok, jnp.exp(s), 0.0)
                dprob = dot_nt(v, ds_[head])
                ds = (p * (dprob - delta[head])).astype(BF)
                ps.append(p.astype(BF))
                dss.append(ds)
                new.append(dqt[head] + dot(kt_ref[kb, head * HEAD:(head + 1) * HEAD, :], ds))
            acc_scr[kr, 0:128] += dot(jnp.concatenate(dss, axis=1), q_two)
            acc_scr[kr, 128:256] += dot(jnp.concatenate(ps, axis=1), do_two)
            return tuple(new)

        zero = jnp.zeros((HEAD, tile), F32)
        dqt = lax.fori_loop(low, qb + 1, step, (zero, zero))
        dps_scr[qr, 0:128] = (jnp.concatenate(dqt, axis=0).T * 0.125).astype(BF)

    own = own_ref[...]
    own_start = doc_starts(own, ends_ref)
    q16 = q16_ref[...]
    do16 = do16_ref[...]
    both = jnp.concatenate([q16, do16], axis=0)
    delta16 = jnp.sum((do16.astype(F32) * o16_ref[...]).T, axis=0, keepdims=True)
    lse16 = lse16_ref[...]

    def step16(kb, dq):
        kr = rows(kb, tile)
        kv = sp_ref[kr, 384:512]
        kpos = iota((tile, tile), 0) + kb * tile
        ok = (kpos <= own) & (kpos >= own_start)
        p = jnp.where(ok, jnp.exp(dot_nt(kv, q16) * 0.125 - lse16), 0.0)
        ds = (p * (dot_nt(kv, do16) - delta16)).astype(BF)
        acc16_scr[kr, :] = dot(jnp.concatenate([ds, p.astype(BF)], axis=1), both)
        return dq + dot_tn(ds, kv)

    dq16 = lax.fori_loop(0, blocks, step16, jnp.zeros((tile, 128), F32))
    dq16_ref[...] = (dq16 * 0.125).astype(BF)

    @pl.loop(0, blocks)
    def _(b):
        r = rows(b, tile)
        dps_scr[r, 128:256] = (acc_scr[r, 0:128] * 0.125).astype(BF)
        dps_scr[r, 256:384] = acc_scr[r, 128:256].astype(BF)
        part = acc16_scr[r, :]
        dps_scr[r, 384:512] = jnp.where(iota(part.shape, 1) < HEAD, part * 0.125, part).astype(BF)

    @pl.loop(0, blocks)
    def _(b):
        r = rows(b, tile)
        pick = jnp.where(scol_ref[r, :] == iota((tile, total), 1), 1.0, 0.0).astype(BF)
        dp_ref[r, :] = dot(pick, dps_scr[...]).astype(BF)


VM = pl.BlockSpec(memory_space=pltpu.VMEM)
SM = pl.BlockSpec(memory_space=pltpu.SMEM)


def attention_forward(ends, me, h_all, w_own, b_own, slots_all, slot):
    total, tile = h_all.shape[0], slot.shape[0]
    blocks = total // tile
    shapes = (
        jax.ShapeDtypeStruct((total, 512), BF),
        jax.ShapeDtypeStruct((blocks, 128, tile), BF),
        jax.ShapeDtypeStruct((total, 128), BF),
        jax.ShapeDtypeStruct((total, 128), F32),
        jax.ShapeDtypeStruct((blocks, 2, tile), F32),
        jax.ShapeDtypeStruct((tile, 128), BF),
        jax.ShapeDtypeStruct((tile, 128), F32),
        jax.ShapeDtypeStruct((1, tile), F32),
    )
    return pl.pallas_call(
        forward_kernel,
        out_shape=shapes,
        in_specs=[SM, SM] + [VM] * 6,
        out_specs=[VM] * len(shapes),
        scratch_shapes=[
            pltpu.VMEM((total, 640), BF),
            pltpu.VMEM((blocks, 256, tile), BF),
            pltpu.VMEM((total, 128), BF),
        ],
        compiler_params=pltpu.CompilerParams(vmem_limit_bytes=40 * 2**20),
        cost_estimate=pl.CostEstimate(flops=14_000_000_000, bytes_accessed=12_000_000, transcendentals=6_000_000),
    )(ends, me, h_all, w_own, b_own, slots_all.reshape(1, total), slots_all.reshape(total, 1), slot.reshape(1, tile))


def attention_backward(ends, slots_all, slot, saved, do, do16):
    sp, kt, of, lse, q16, o16, lse16 = saved
    total, tile = sp.shape[0], slot.shape[0]
    shapes = (jax.ShapeDtypeStruct((total, 512), BF), jax.ShapeDtypeStruct((tile, 128), BF))
    return pl.pallas_call(
        backward_kernel,
        out_shape=shapes,
        in_specs=[SM] + [VM] * 12,
        out_specs=[VM] * len(shapes),
        scratch_shapes=[
            pltpu.VMEM((total, 128), BF),
            pltpu.VMEM((total, 256), F32),
            pltpu.VMEM((total, 128), F32),
            pltpu.VMEM((total, 512), BF),
        ],
        compiler_params=pltpu.CompilerParams(vmem_limit_bytes=40 * 2**20),
        cost_estimate=pl.CostEstimate(flops=20_000_000_000, bytes_accessed=12_000_000, transcendentals=6_000_000),
    )(
        ends, slots_all.reshape(1, total), slots_all.reshape(total, 1), slot.reshape(1, tile),
        sp, kt, of, lse, do, q16, do16, o16, lse16,
    )


def swap(values, axis):
    return lax.ppermute(values, axis, [(0, 1), (1, 0)])


def gather_rep(values):
    other = swap(values, "x")
    pair = jnp.concatenate([values, other], axis=0)
    return jnp.concatenate([pair, swap(pair, "core")], axis=0)


def scatter_rep(parts):
    half = parts.shape[0] // 2
    pair = parts[:half] + swap(parts[half:].astype(BF), "core").astype(F32)
    quarter = half // 2
    return pair[:quarter] + swap(pair[quarter:].astype(BF), "x").astype(F32)


def in_order(mine, other, axis):
    first = lax.axis_index(axis) == 0
    return jnp.where(first, mine, other), jnp.where(first, other, mine)


def ordered_rep(values):
    pair = jnp.stack(in_order(values, swap(values, "x"), "x"))
    first, second = in_order(pair, swap(pair, "core"), "core")
    return jnp.stack([first, second])


def split_rep(values):
    half = values.shape[1] // 2
    keep, send = in_order(values[:, :half], values[:, half:], "core")
    kept = keep + swap(send.astype(BF), "core").astype(F32)
    half = half // 2
    keep, send = in_order(kept[:, :half], kept[:, half:], "x")
    return keep + swap(send.astype(BF), "x").astype(F32)


def sum_rep(values):
    for axis in ("core", "x"):
        low = values.astype(BF)
        values = low.astype(F32) + swap(low, axis).astype(F32)
    return values


def sum_all(values):
    z_size = lax.axis_size("z")
    for axis in ("core", "x", "y"):
        values = values + swap(values, axis)
    step = 1
    while step < z_size:
        values = values + lax.ppermute(values, "z", [(n, n ^ step) for n in range(z_size)])
        step = step * 2
    return sum_dp(values)


def sum_dp(values):
    if lax.axis_size("dp") > 1:
        return lax.psum(values, "dp")
    return values


def gather_shard(values):
    return lax.all_gather(values, SHARD, axis=0, tiled=True)


def scatter_shard(values):
    return lax.psum_scatter(values.astype(BF), SHARD, scatter_dimension=0, tiled=True)


def exchange_shard(values):
    return lax.all_to_all(values, SHARD, 0, 0, tiled=True)


def norm_stats(values):
    centre = values - jnp.mean(values, axis=-1, keepdims=True)
    spread = jnp.mean(centre * centre, axis=-1, keepdims=True)
    rate = lax.rsqrt(spread + 1e-05)
    return centre * rate, rate


def norm_back(grad, normed, rate, gain):
    scaled = grad * gain
    inner = jnp.mean(scaled * normed, axis=-1, keepdims=True)
    back = rate * (scaled - jnp.mean(scaled, axis=-1, keepdims=True) - normed * inner)
    return back, jnp.sum(grad * normed, axis=0), jnp.sum(grad, axis=0)


def gelu_tanh(values):
    return jax.nn.gelu(values, approximate=True)


def shards(
    tokens, slot, lengths, attn_in_weight, attn_out_weight, up_weight, down_weight,
    norm_gains, layer_biases, up_bias, cotangent,
):
    tile, feats = tokens.shape
    n_shard = lax.axis_size("z") * lax.axis_size("y")
    heads = feats // HEAD
    per = heads // n_shard
    mine = per * HEAD
    spare = n_shard * mine
    me = lax.axis_index("z") * lax.axis_size("y") + lax.axis_index("y")
    rep = lax.axis_index("x") * 2 + lax.axis_index("core")
    row_part = attn_in_weight.shape[0]
    ff_part = down_weight.shape[0]
    n_rep = 4
    quarter = ff_part // n_rep

    in_parts = attn_in_weight.reshape(row_part, 3, feats)
    main = in_parts[:, :, :spare].reshape(row_part, 3, n_shard, mine).transpose(2, 0, 1, 3)
    main = main.reshape(n_shard, row_part, 3 * mine)
    extra = jnp.concatenate([in_parts[:, 1, spare:], in_parts[:, 2, spare:], in_parts[:, 0, spare:]], axis=1)
    extra = jnp.broadcast_to(extra[None], (n_shard,) + extra.shape)
    w_own = exchange_shard(jnp.concatenate([main, extra], axis=2)).reshape(feats, -1)
    w_pad = jnp.pad(w_own, ((0, 0), (0, 640 - w_own.shape[1])))

    ends = jnp.cumsum(lengths[0]).astype(jnp.int32)
    slots_all = gather_shard(slot)

    tokens_f = tokens.astype(F32)
    normed1, rate1 = norm_stats(tokens_f)
    h_first = (normed1 * norm_gains[0] + layer_biases[0]).astype(BF)
    h_all = gather_shard(h_first)

    up_mine = lax.dynamic_index_in_dim(
        up_weight.reshape(row_part, n_shard, n_rep, quarter), rep, 2, keepdims=False
    ).reshape(row_part, n_shard * quarter)
    down_mine = lax.dynamic_slice_in_dim(down_weight, rep * quarter, quarter, 0)
    w_out = gather_shard(attn_out_weight)
    w_ff = gather_shard(jnp.concatenate([up_mine, down_mine], axis=1))
    w_up, w_down = w_ff[:, : n_shard * quarter], w_ff[:, n_shard * quarter :]
    up_bias_mine = lax.dynamic_index_in_dim(
        up_bias.reshape(n_shard, n_rep, quarter), rep, 1, keepdims=False
    ).reshape(-1)

    query_bias = lax.dynamic_slice_in_dim(layer_biases[1], me * mine, mine)
    value_bias = lax.dynamic_slice_in_dim(layer_biases[2], me * mine, mine)
    zeros = functools.partial(jnp.zeros, dtype=F32)
    b_own = jnp.concatenate(
        [query_bias, zeros(mine), value_bias, zeros(HEAD), layer_biases[2, spare:], layer_biases[1, spare:], zeros(HEAD)]
    )[None]

    sp, kt, o_own, of, lse, q16, o16, lse16 = attention_forward(
        ends, me.reshape(1).astype(jnp.int32), h_all, w_pad, b_own, slots_all, slot
    )
    o_back = exchange_shard(o_own.reshape(n_shard, tile, mine))
    attended = jnp.concatenate(
        [o_back.transpose(1, 0, 2).reshape(tile, spare), o16[:, HEAD:].astype(BF)], axis=1
    )
    middle = tokens_f + dot(attended, w_out) + layer_biases[3]
    normed2, rate2 = norm_stats(middle)
    h_second = (normed2 * norm_gains[1] + layer_biases[4]).astype(BF)

    dout_rep = gather_rep(cotangent)
    h_rep = gather_rep(h_second)
    pre = dot(h_rep, w_up) + up_bias_mine
    act_f, gelu_back = jax.vjp(gelu_tanh, pre)
    act = act_f.astype(BF)
    mixed = (middle + scatter_rep(dot(act, w_down)) + layer_biases[5]).astype(BF)

    dpre = gelu_back(dot_nt(dout_rep, w_down))[0].astype(BF)
    dh_second = scatter_rep(dot_nt(dpre, w_up))
    down_grad = dot_tn(act, dout_rep)
    up_grad = dot_tn(h_rep, dpre)
    up_bias_grad = jnp.sum(dpre.astype(F32), axis=0)

    dout = cotangent.astype(F32)
    norm_grad, gain_two, bias_two = norm_back(dh_second, normed2, rate2, norm_gains[1])
    dmiddle = dout + norm_grad
    dbranch = dmiddle.astype(BF)
    dattended = dot_nt(dbranch, w_out).astype(BF)
    out_grad = split_rep(dot_tn(attended, dbranch))
    owned = scatter_shard(jnp.concatenate([up_grad, down_grad, out_grad], axis=1))

    do_own = exchange_shard(dattended[:, :spare].reshape(tile, n_shard, mine).transpose(1, 0, 2))
    do16 = jnp.pad(dattended[:, spare:], ((0, 0), (HEAD, 0)))
    dp, dq16 = attention_backward(
        ends, slots_all, slot, (sp, kt, of, lse, q16, o16, lse16), do_own.reshape(-1, mine), do16
    )
    dq16 = dq16[:, :HEAD]
    dh_first = scatter_shard(dot_nt(dp, w_own[:, :512])).astype(F32) + dot_nt(dq16, w_own[:, 512:])
    in_grad = jnp.concatenate([dot_tn(h_all, dp), dot_tn(h_first, dq16)], axis=1).astype(BF)
    in_back = exchange_shard(in_grad.reshape(n_shard, row_part, -1))
    norm_grad, gain_one, bias_one = norm_back(dh_first, normed1, rate1, norm_gains[0])
    tokens_grad = dmiddle + norm_grad

    in_main = in_back[:, :, : 3 * mine].reshape(n_shard, row_part, 3, mine).transpose(1, 2, 0, 3)
    in_main = in_main.reshape(row_part, 3, spare)
    in_extra = jnp.sum(in_back[:, :, 3 * mine :].astype(F32), axis=0).astype(BF)
    key16, value16, query16 = jnp.split(in_extra, 3, axis=1)
    in_rows = jnp.concatenate([in_main, jnp.stack([query16, key16, value16], axis=1)], axis=2)
    in_out = sum_dp(sum_rep(in_rows.reshape(row_part, 3 * feats)))

    owned = sum_dp(owned)
    whole = ordered_rep(owned)
    wide = n_shard * quarter
    up_out = whole[..., :wide].reshape(2, 2, row_part, n_shard, quarter).transpose(2, 3, 1, 0, 4)
    up_out = up_out.reshape(row_part, -1).astype(F32)
    down_out = whole[..., wide : 2 * wide].transpose(1, 0, 2, 3).reshape(ff_part, feats).astype(F32)
    out_out = whole[..., 2 * wide :].transpose(2, 0, 1, 3).reshape(row_part, feats).astype(F32)

    dp_sums = jnp.sum(dp.astype(F32), axis=0)
    query_sums = lax.dynamic_update_slice(zeros(feats), dp_sums[:mine], (me * mine,))
    query_sums = query_sums + jnp.pad(jnp.sum(dq16.astype(F32), axis=0), (spare, 0))
    value_sums = lax.dynamic_update_slice(zeros(feats), dp_sums[2 * mine : 3 * mine], (me * mine,))
    value_sums = value_sums + jnp.pad(dp_sums[3 * mine + HEAD : 3 * mine + 2 * HEAD], (spare, 0))
    place = (jnp.arange(n_rep) == rep)[:, None]
    vectors = jnp.concatenate(
        [
            jnp.stack(
                [
                    bias_one, query_sums, value_sums, jnp.sum(dbranch.astype(F32), axis=0),
                    bias_two, jnp.sum(dout, axis=0), gain_one, gain_two,
                ]
            ),
            jnp.where(place, up_bias_grad[None], 0.0),
        ]
    )
    vectors = lax.dynamic_slice_in_dim(sum_all(vectors), me * row_part, row_part, 1)
    return (
        mixed, tokens_grad, in_out, out_out, up_out, down_out,
        vectors[6:8], vectors[0:6], vectors[8:].reshape(-1),
    )


def solution(mesh):
    replicas, n_shard = mesh.shape["replica"], mesh.shape["shard"]
    fine = Mesh(
        mesh.devices.reshape(replicas // 4, 2, 2, n_shard // 2, 2), ("dp", "x", "core", "z", "y")
    )
    rep = ("dp", "x", "core")
    both = rep + SHARD
    in_specs = (
        P(both, None), P(both), P(rep, None), P(SHARD, None), P(SHARD, None), P(SHARD, None), P(SHARD, None),
        P(), P(), P(), P(both, None),
    )
    out_specs = (
        P(both, None), P(both, None), P(SHARD, None), P(SHARD, None), P(SHARD, None), P(SHARD, None),
        P(None, SHARD), P(None, SHARD), P(SHARD),
    )
    return jax.shard_map(shards, mesh=fine, in_specs=in_specs, out_specs=out_specs, check_vma=False)
```

time: 2310 us -> 739 us (0.32)
  waiting for transfers between devices: 1500 us -> 319 us
  local copies, waits for them, and re-layouts: 472 us -> 148 us
  matrix products: 192 us -> 56.7 us
  Pallas kernels: 0 us -> 70 us
  other arithmetic: 71.3 us -> 39.1 us
  starting transfers between devices: 0.53 us -> 32 us
    unnamed x12 -> x5, waiting for transfers between devices: 969 us -> 0.76 us
    all_gather x5 -> x3, waiting for transfers between devices: 464 us -> 81.1 us  [gather_shard(): return lax.all_gather(values, SHARD, axis=0, tiled=True)]
    dot_general x40 -> x13, matrix products: 192 us -> 56.7 us  [the longest x5 22.1 us: dot_nt(): lax.dot_general(left, right, (((1,), (1,)), ((), ())), preferred_element_...]
    convert_element_type x2 -> x8, local copies, waits for them, and re-layouts: 151 us -> 33.2 us  [the longest x3 20.4 us: shards(): up_out = up_out.reshape(row_part, -1).astype(F32)]
    reshape x24 -> x12, local copies, waits for them, and re-layouts: 88.7 us -> 17.5 us  [the longest x1 7.31 us: shards(): up_weight.reshape(row_part, n_shard, n_rep, quarter)]
    pallas_call x0 -> x2, Pallas kernels: none -> 70 us  [the longest x1 36.5 us: attention_forward(): pl.pallas_call(forward_kernel, out_shape=shapes, in_specs=[SM, SM] + [VM]...]
    ppermute x0 -> x19, waiting for transfers between devices: none -> 67.1 us  [the longest x17 63 us: swap(): return lax.ppermute(values, axis, [(0, 1), (1, 0)])]
    all_to_all x0 -> x4, waiting for transfers between devices: none -> 55 us  [exchange_shard(): return lax.all_to_all(values, SHARD, 0, 0, tiled=True)]
  transfers between devices with their start and end apart: 9 -> 28, of which waited for: 8 -> 19; matrix products, arithmetic and copies ran while one was open for 8% -> 20% of each run, Pallas kernels for 0% -> 5%
where the time goes in v1:
time: 739 us; the launch traced here: 727 us
  waiting for transfers between devices  319 us (43%)
  local copies, waits for them, and re-layouts  148 us (20%)
  Pallas kernels  70 us (9%)
  matrix products  56.7 us (8%)
  blocking collectives  47.7 us (6%)
  other arithmetic  39.1 us (5%)
  starting transfers between devices  32 us (4%)
  between operations  15.2 us (2%)
    reduce_scatter x2, waiting for transfers between devices, scatter_shard(): lax.psum_scatter(values.astype(BF), SHARD, scatter_dimension=0, tiled=True)  115 us
    all_gather x3, waiting for transfers between devices, gather_shard(): return lax.all_gather(values, SHARD, axis=0, tiled=True)  81.1 us
    ppermute x17, waiting for transfers between devices, swap(): return lax.ppermute(values, axis, [(0, 1), (1, 0)])  63 us
    all_to_all x4, waiting for transfers between devices, exchange_shard(): return lax.all_to_all(values, SHARD, 0, 0, tiled=True)  55 us
    all_gather x1, blocking collectives, gather_shard(): return lax.all_gather(values, SHARD, axis=0, tiled=True)  47.7 us
    unnamed x110, local copies, waits for them, and re-layouts  41.9 us
    pallas_call x1, Pallas kernels, attention_forward(): pl.pallas_call(forward_kernel, out_shape=shapes, in_specs=[SM, SM] + [VM]...  36.5 us
    pallas_call x1, Pallas kernels, attention_backward(): pl.pallas_call(backward_kernel, out_shape=shapes, in_specs=[SM] + [VM] *...  33.5 us
  transfers between devices with their start and end apart: 28, of which 19 were waited for; matrix products, arithmetic and copies ran while one was open for 20% of the time, Pallas kernels for 5%

profile of v1, /device:TPU:0, one launch (start us, length us, event | category | flops | bytes accessed | tf_op | source)
XLA Modules:
  0.0 727.0 jit_solution(2212160560041116067)
XLA Ops:
  13.2 7.3 %reshape.189 = bf16[136,8,4,136]{3,2,1,0:T(4,128)(2,1)} reshape(bf16[136,4352]{1,0:T(8,128)(2,1)S(1)} %copy-done.28) | data formatting | bytes 2367488 | tf_op jit(solution)/shard_map/reshape | solution.py:421
  32.0 7.6 %all-to-all-start = ((bf16[8,136,576]{2,1,0:T(8,128)(2,1)}), bf16[8,136,576]{2,1,0:T(8,128)(2,1)S(1)}, u32[]{:S(2)}, u32[]{:S(2)}) async-start(bf16[8,136,576]{2,1,0:T(8,128)(2,1)} %pad_maximum_fusion.1), calls=%async_computation | async-start | bytes 2785280 | tf_op jit(solution)/shard_map/all_to_all | solution.py:366
  40.7 47.7 %all-gather = s32[8,1,256]{2,1,0:T(1,128)S(1)} all-gather(s32[1,1,256]{2,1,0:T(1,128)S(1)} %bitcast.81), channel_id=1, replica_groups=mesh['dp'=1,'x'=2,'core'=2,'z'=4,'y'=2] {'z','y'}, dimensions={0}, use_global_device_ids=true | all-gather | bytes 9216 | tf_op jit(solution)/shard_map/all_gather | solution.py:358
  88.8 6.9 all-to-all-done
  98.2 16.6 %all-gather.5.cloned.1.call-done.h_ref = bf16[2048,1088]{1,0:T(8,128)(2,1)} async-done(((bf16[256,1088]{1,0:T(8,128)(2,1)}), bf16[2048,1088]{1,0:T(8,128)(2,1)}) %all-gather.5.cloned.1.call-update) | async-done | bytes 4456464 | tf_op jit(solution)/shard_map/all_gather | solution.py:358
  117.2 36.5 %shard_map.178 = (bf16[2048,512]{1,0:T(8,128)(2,1)S(1)}, bf16[8,128,256]{2,1,0:T(8,128)(2,1)S(1)}, bf16[2048,128]{1,0:T(8,128)(2,1)S(1)}, f32[2048,128]{1,0:T(8,...) custom-call(s32[6]{0:T(128)S(1)} %bitcast.84, ...), custom_call_target="tpu_custom_call" | custom-call | flops 14000000000 | bytes 12000000 | tf_op jit(solution)/shard_map/pallas_call | solution.py:258
  161.6 17.2 %all-gather.7.cloned.1.call-done = bf16[1088,1088]{1,0:T(8,128)(2,1)} async-done(((bf16[136,1088]{1,0:T(8,128)(2,1)}), bf16[1088,1088]{1,0:T(8,128)(2,1)}) %all-gather.7.cloned.1.call-update) | async-done | bytes 2367504 | tf_op jit(solution)/shard_map/all_gather | solution.py:358
  188.7 10.6 %collective-permute-done = bf16[256,1088]{0,1:T(8,128)(2,1)} collective-permute-done((bf16[256,1088]{0,1:T(8,128)(2,1)}, bf16[256,1088]{0,1:T(8,128)(2,1)}, u32[]{:S(2)}, u32[]{:S(2)}) %collective-permute-start) | collective-permute-done | bytes 557088 | tf_op jit(solution)/shard_map/ppermute | solution.py:297
  212.5 47.3 %all-gather.9.cloned.1.call-done = bf16[1088,2176]{1,0:T(8,128)(2,1)} async-done(((bf16[136,2176]{1,0:T(8,128)(2,1)}), bf16[1088,2176]{1,0:T(8,128)(2,1)}) %all-gather.9.cloned.1.call-update) | async-done | bytes 4734992 | tf_op jit(solution)/shard_map/all_gather | solution.py:358
  265.4 10.6 %convert_reduce_fusion = (f32[1088]{0:T(1024)}, bf16[1024,1088]{0,1:T(8,128)(2,1)S(1)}) fusion(f32[1024,1088]{0,1:T(8,128)S(1)} %convolution_add_fusion, bf16[1024,1088]{0,1:T(8,128)(2,1)} %constant_dynamic-update-slice_fusion, bf16[1088,2176]{1,0:T(8,128)(2,1)S(1)} %copy-done.45), kind=kOutput, calls=%fused_computation.13 | convolution fusion | flops 2448817152 | bytes 11424000 | tf_op jit(solution)/shard_map/dot_general | solution.py:23
  319.8 6.5 collective-permute-done.7
  330.1 7.1 collective-permute-done.3
  349.4 13.9 %all-to-all-done.2 = bf16[8,256,128]{2,1,0:T(8,128)(2,1)S(1)} async-done(((bf16[8,256,128]{2,1,0:T(8,128)(2,1)}), bf16[8,256,128]{2,1,0:T(8,128)(2,1)S(1)}, u32[]{:S(2)}, u32[]{:S(2)}) %all-to-all-start.2) | async-done | bytes 524320 | tf_op jit(solution)/shard_map/all_to_all | solution.py:366
  369.0 33.5 %shard_map.179 = (bf16[2048,512]{1,0:T(8,128)(2,1)S(1)}, bf16[256,128]{1,0:T(8,128)(2,1)S(1)}) custom-call(s32[6]{0:T(128)S(1)} %bitcast.85, s32[1,2048]{1,0:T(1,128)S(1)} %bitcast.80, s32[2048,1]{1,0:T(8,128)S(1)} %copy.198.scol_ref, s32[1,256]{1,0:T(1,128)S(1)} %bitcast.83, bf16[2048,512]{1,0:T(8,128)(2,1)S(1)} %copy-done.7, ...), custom_call_target="tpu_custom_call" | custom-call | flops 20000000000 | bytes 12000000 | tf_op jit(solution)/shard_map/pallas_call | solution.py:277
  407.1 6.5 copy.219
  426.7 8.6 %convolution_convert_fusion = bf16[1088,1088]{1,0:T(8,128)(2,1)} fusion(bf16[1024,1088]{0,1:T(8,128)(2,1)} %constant_dynamic-update-slice_fusion, f32[1024,1088]{0,1:T(8,128)} %copy-done.48), kind=kOutput, calls=%fused_computation | convolution fusion | flops 2435518464 | bytes 9052160 | tf_op jit(solution)/shard_map/dot_general | solution.py:27
  445.3 9.9 %concatenate.61 = bf16[1088,2448]{1,0:T(8,128)(2,1)} concatenate(bf16[1088,1088]{1,0:T(8,128)(2,1)} %convolution_convert_fusion.1, bf16[1088,1088]{1,0:T(8,128)(2,1)} %convolution_convert_fusion, bf16[1088,272]{1,0:T(8,128)(2,1)S(1)} %copy.226), dimensions={1} | concatenate | bytes 10653696 | tf_op jit(solution)/shard_map/concatenate | solution.py:468
  468.2 33.0 %all-to-all-done.3 = bf16[8,136,576]{2,1,0:T(8,128)(2,1)} async-done(((bf16[8,136,576]{2,1,0:T(8,128)(2,1)}), bf16[8,136,576]{2,1,0:T(8,128)(2,1)}, u32[]{:S(2)}, u32[]{:S(2)}) %all-to-all-start.3) | async-done | bytes 1253408 | tf_op jit(solution)/shard_map/all_to_all | solution.py:366
  515.3 6.5 reduce-scatter.3.cloned.1.call-done
  524.8 108.1 %reduce-scatter.5.cloned.1.call-done = bf16[136,2448]{1,0:T(8,128)(2,1)} async-done(((bf16[1088,2448]{1,0:T(8,128)(2,1)}), bf16[136,2448]{1,0:T(8,128)(2,1)}) %reduce-scatter.5.cloned.1.call-update) | async-done | bytes 665872 | tf_op jit(solution)/shard_map/reduce_scatter | solution.py:362
  637.9 13.7 %collective-permute-done.12 = bf16[136,2448]{1,0:T(8,128)(2,1)S(1)} collective-permute-done((bf16[136,2448]{1,0:T(8,128)(2,1)}, bf16[136,2448]{1,0:T(8,128)(2,1)S(1)}, u32[]{:S(2)}, u32[]{:S(2)}) %collective-permute-start.12) | collective-permute-done | bytes 665888 | tf_op jit(solution)/shard_map/ppermute | solution.py:297
  652.9 17.5 %collective-permute-done.9 = bf16[136,3264]{1,0:T(8,128)(2,1)S(1)} collective-permute-done((bf16[136,3264]{1,0:T(8,128)(2,1)S(1)}, bf16[136,3264]{1,0:T(8,128)(2,1)S(1)}, u32[]{:S(2)}, u32[]{:S(2)}) %collective-permute-start.9) | collective-permute-done | bytes 887840 | tf_op jit(solution)/shard_map/ppermute | solution.py:297
  705.6 7.9 %copy.228 = f32[136,8,2,2,136]{4,3,2,1,0:T(2,128)} copy(f32[136,8,2,2,136]{4,1,0,2,3:T(8,128)} %bitcast.86) | data formatting | bytes 4734976 | tf_op jit(solution)/shard_map/convert_element_type | solution.py:493
  713.5 6.5 reshape.199
  (296 shorter events, 224.3 us)
Async XLA Ops:
  7.2 107.6 %all-gather.5.cloned.1.call-start = ((), (), s32[]{:S(2)}) async-start(), calls=%async_computation.6 | async-start | bytes 5308416 | tf_op jit(solution)/shard_map/all_gather | solution.py:358
  12.4 166.5 %all-gather.7.cloned.1.call-start = ((), (), s32[]{:S(2)}) async-start(), calls=%async_computation.7 | async-start | bytes 2820096 | tf_op jit(solution)/shard_map/all_gather | solution.py:358
  13.1 246.7 %all-gather.9.cloned.1.call-start = ((), (), s32[]{:S(2)}) async-start(), calls=%async_computation.8 | async-start | bytes 5326848 | tf_op jit(solution)/shard_map/all_gather | solution.py:358
  32.0 63.7 %all-to-all-start = ((bf16[8,136,576]{2,1,0:T(8,128)(2,1)}), bf16[8,136,576]{2,1,0:T(8,128)(2,1)S(1)}, u32[]{:S(2)}, u32[]{:S(2)}) async-start(bf16[8,136,576]{2,1,0:T(8,128)(2,1)} %pad_maximum_fusion.1), calls=%async_computation | async-start | bytes 2785280 | tf_op jit(solution)/shard_map/all_to_all | solution.py:366
  157.8 22.3 %all-to-all-start.1 = ((bf16[8,256,128]{1,2,0:T(8,128)(2,1)}), bf16[8,256,128]{1,2,0:T(8,128)(2,1)S(1)}, u32[]{:S(2)}, u32[]{:S(2)}) async-start(bf16[8,256,128]{1,2,0:T(8,128)(2,1)} %copy.199), calls=%async_computation.1 | async-start | bytes 1048576 | tf_op jit(solution)/shard_map/all_to_all | solution.py:366
  161.3 25.0 %collective-permute-start.4 = (bf16[256,1088]{0,1:T(8,128)(2,1)}, bf16[256,1088]{0,1:T(8,128)(2,1)}, u32[]{:S(2)}, u32[]{:S(2)}) collective-permute-start(bf16[256,1088]{0,1:T(8,128)(2,1)} %param.21), channel_id=1, source_target_pairs={{0,16},{16,0},{1,17},{17,1},{2,18},{18,2},{3,19},{19,3},{4,20},{20... | collective-permute-start | bytes 1671176 | tf_op jit(solution)/shard_map/ppermute | solution.py:297
  184.9 14.4 %collective-permute-start = (bf16[256,1088]{0,1:T(8,128)(2,1)}, bf16[256,1088]{0,1:T(8,128)(2,1)}, u32[]{:S(2)}, u32[]{:S(2)}) collective-permute-start(bf16[256,1088]{0,1:T(8,128)(2,1)} %copy.205), channel_id=1, source_target_pairs={{0,16},{16,0},{1,17},{17,1},{2,18},{18,2},{3,19},{19,3},{4,20},{20... | collective-permute-start | bytes 1671176 | tf_op jit(solution)/shard_map/ppermute | solution.py:297
  188.7 21.5 %collective-permute-start.5 = (bf16[512,1088]{0,1:T(8,128)(2,1)}, bf16[512,1088]{0,1:T(8,128)(2,1)}, u32[]{:S(2)}, u32[]{:S(2)}) collective-permute-start(bf16[512,1088]{0,1:T(8,128)(2,1)} %pad_maximum_fusion.6), channel_id=1, source_target_pairs={{0,8},{8,0},{1,9},{9,1},{2,10},{10,2},{3,11},{11,3},{4,12},{12,4},... | collective-permute-start | bytes 3342344 | tf_op jit(solution)/shard_map/ppermute | solution.py:297
  205.9 53.9 %collective-permute-start.1 = (bf16[512,1088]{0,1:T(8,128)(2,1)}, bf16[512,1088]{0,1:T(8,128)(2,1)}, u32[]{:S(2)}, u32[]{:S(2)}) collective-permute-start(bf16[512,1088]{0,1:T(8,128)(2,1)} %copy.204), channel_id=1, source_target_pairs={{0,8},{8,0},{1,9},{9,1},{2,10},{10,2},{3,11},{11,3},{4,12},{12,4},... | collective-permute-start | bytes 3342344 | tf_op jit(solution)/shard_map/ppermute | solution.py:297
  282.4 21.0 %collective-permute-start.6 = (bf16[512,1088]{0,1:T(8,128)(2,1)}, bf16[512,1088]{0,1:T(8,128)(2,1)}, u32[]{:S(2)}, u32[]{:S(2)}) collective-permute-start(bf16[512,1088]{0,1:T(8,128)(2,1)} %slice.281), channel_id=1, source_target_pairs={{0,8},{8,0},{1,9},{9,1},{2,10},{10,2},{3,11},{11,3},{4,12},{12,4},... | collective-permute-start | bytes 3342344 | tf_op jit(solution)/shard_map/ppermute | solution.py:297
  289.8 22.1 %collective-permute-start.2 = (bf16[512,1088]{0,1:T(8,128)(2,1)}, bf16[512,1088]{0,1:T(8,128)(2,1)}, u32[]{:S(2)}, u32[]{:S(2)}) collective-permute-start(bf16[512,1088]{0,1:T(8,128)(2,1)} %slice.282), channel_id=1, source_target_pairs={{0,8},{8,0},{1,9},{9,1},{2,10},{10,2},{3,11},{11,3},{4,12},{12,4},... | collective-permute-start | bytes 3342344 | tf_op jit(solution)/shard_map/ppermute | solution.py:297
  310.5 15.8 %collective-permute-start.7 = (bf16[256,1088]{0,1:T(8,128)(2,1)}, bf16[256,1088]{0,1:T(8,128)(2,1)}, u32[]{:S(2)}, u32[]{:S(2)}) collective-permute-start(bf16[256,1088]{0,1:T(8,128)(2,1)} %copy.214), channel_id=1, source_target_pairs={{0,16},{16,0},{1,17},{17,1},{2,18},{18,2},{3,19},{19,3},{4,20},{20... | collective-permute-start | bytes 1671176 | tf_op jit(solution)/shard_map/ppermute | solution.py:297
  319.2 18.0 %collective-permute-start.3 = (bf16[256,1088]{0,1:T(8,128)(2,1)}, bf16[256,1088]{0,1:T(8,128)(2,1)}, u32[]{:S(2)}, u32[]{:S(2)}) collective-permute-start(bf16[256,1088]{0,1:T(8,128)(2,1)} %copy.209), channel_id=1, source_target_pairs={{0,16},{16,0},{1,17},{17,1},{2,18},{18,2},{3,19},{19,3},{4,20},{20... | collective-permute-start | bytes 1671176 | tf_op jit(solution)/shard_map/ppermute | solution.py:297
  345.7 17.6 %all-to-all-start.2 = ((bf16[8,256,128]{2,1,0:T(8,128)(2,1)}), bf16[8,256,128]{2,1,0:T(8,128)(2,1)S(1)}, u32[]{:S(2)}, u32[]{:S(2)}) async-start(bf16[8,256,128]{2,1,0:T(8,128)(2,1)} %bitcast_bitcast_fusion), calls=%async_computation.2 | async-start | bytes 1048576 | tf_op jit(solution)/shard_map/all_to_all | solution.py:366
  349.2 172.5 %reduce-scatter.3.cloned.1.call-start = ((), (), s32[]{:S(2)}) async-start(), calls=%async_computation.9 | async-start | bytes 5308416 | tf_op jit(solution)/shard_map/reduce_scatter | solution.py:362
  413.7 219.2 %reduce-scatter.5.cloned.1.call-start = ((), (), s32[]{:S(2)}) async-start(), calls=%async_computation.10 | async-start | bytes 6266880 | tf_op jit(solution)/shard_map/reduce_scatter | solution.py:362
  426.6 16.2 %collective-permute-start.11 = (bf16[1088,272]{0,1:T(8,128)(2,1)S(1)}, bf16[1088,272]{0,1:T(8,128)(2,1)S(1)}, u32[]{:S(2)}, u32[]{:S(2)}) collective-permute-start(bf16[1088,272]{0,1:T(8,128)(2,1)S(1)} %select_convert_fusion.1), channel_id=1, source_target_pairs={{0,16},{16,0},{1,17},{17,1},{2,18},{18,2},{3,19},{19,3},{4,20},{20... | collective-permute-start | bytes 1775624 | tf_op jit(solution)/shard_map/ppermute | solution.py:297
  463.6 37.5 %all-to-all-start.3 = ((bf16[8,136,576]{2,1,0:T(8,128)(2,1)}), bf16[8,136,576]{2,1,0:T(8,128)(2,1)}, u32[]{:S(2)}, u32[]{:S(2)}) async-start(bf16[8,136,576]{2,1,0:T(8,128)(2,1)} %pad_maximum_fusion.2), calls=%async_computation.4 | async-start | bytes 2785280 | tf_op jit(solution)/shard_map/all_to_all | solution.py:366
  512.1 122.2 %collective-permute-start.8 = (bf16[136,3264]{1,0:T(8,128)(2,1)}, bf16[136,3264]{1,0:T(8,128)(2,1)}, u32[]{:S(2)}, u32[]{:S(2)}) collective-permute-start(bf16[136,3264]{1,0:T(8,128)(2,1)} %reshape.196), channel_id=1, source_target_pairs={{0,8},{8,0},{1,9},{9,1},{2,10},{10,2},{3,11},{11,3},{4,12},{12,4},... | collective-permute-start | bytes 2663432 | tf_op jit(solution)/shard_map/ppermute | solution.py:297
  524.7 111.7 %collective-permute-start.14 = (f32[12,1088]{1,0:T(8,128)S(1)}, f32[12,1088]{1,0:T(8,128)S(1)}, u32[]{:S(2)}, u32[]{:S(2)}) collective-permute-start(f32[12,1088]{1,0:T(8,128)S(1)} %concatenate.62), channel_id=1, source_target_pairs={{0,8},{8,0},{1,9},{9,1},{2,10},{10,2},{3,11},{11,3},{4,12},{12,4},... | collective-permute-start | bytes 156680 | tf_op jit(solution)/shard_map/ppermute | solution.py:297
  632.9 18.7 %collective-permute-start.12 = (bf16[136,2448]{1,0:T(8,128)(2,1)}, bf16[136,2448]{1,0:T(8,128)(2,1)S(1)}, u32[]{:S(2)}, u32[]{:S(2)}) collective-permute-start(bf16[136,2448]{1,0:T(8,128)(2,1)} %reduce-scatter.5.cloned.1.call-done), channel_id=1, source_target_pairs={{0,16},{16,0},{1,17},{17,1},{2,18},{18,2},{3,19},{19,3},{4,20},{20... | collective-permute-start | bytes 1997576 | tf_op jit(solution)/shard_map/ppermute | solution.py:297
  635.8 34.7 %collective-permute-start.9 = (bf16[136,3264]{1,0:T(8,128)(2,1)S(1)}, bf16[136,3264]{1,0:T(8,128)(2,1)S(1)}, u32[]{:S(2)}, u32[]{:S(2)}) collective-permute-start(bf16[136,3264]{1,0:T(8,128)(2,1)S(1)} %add_convert_fusion), channel_id=1, source_target_pairs={{0,16},{16,0},{1,17},{17,1},{2,18},{18,2},{3,19},{19,3},{4,20},{20... | collective-permute-start | bytes 2663432 | tf_op jit(solution)/shard_map/ppermute | solution.py:297
  636.4 35.5 %collective-permute-start.15 = (f32[12,1088]{1,0:T(8,128)S(1)}, f32[12,1088]{1,0:T(8,128)S(1)}, u32[]{:S(2)}, u32[]{:S(2)}) collective-permute-start(f32[12,1088]{1,0:T(8,128)S(1)} %add.210), channel_id=1, source_target_pairs={{0,16},{16,0},{1,17},{17,1},{2,18},{18,2},{3,19},{19,3},{4,20},{20... | collective-permute-start | bytes 156680 | tf_op jit(solution)/shard_map/ppermute | solution.py:297
  652.9 36.8 %collective-permute-start.13 = (bf16[2,136,2448]{2,1,0:T(8,128)(2,1)}, bf16[2,136,2448]{2,1,0:T(8,128)(2,1)}, u32[]{:S(2)}, u32[]{:S(2)}) collective-permute-start(bf16[2,136,2448]{2,1,0:T(8,128)(2,1)} %pad_maximum_fusion.3), channel_id=1, source_target_pairs={{0,8},{8,0},{1,9},{9,1},{2,10},{10,2},{3,11},{11,3},{4,12},{12,4},... | collective-permute-start | bytes 3995144 | tf_op jit(solution)/shard_map/ppermute | solution.py:297
  (55 other events, 523.5 us)
Sparse Core Ops, SparseCore 0:
  12.5 102.3 all-gather.4
  117.0 61.7 all-gather.6
  181.6 78.1 all-gather.8
  413.8 107.9 reduce-scatter.2
  525.2 107.5 reduce-scatter.4

commit v2 on v1

v2 whole, which is shorter than its diff:
```python
import functools
import math

import jax
import jax.numpy as jnp
from jax import lax
from jax.experimental import pallas as pl
from jax.experimental.pallas import tpu as pltpu
from jax.sharding import Mesh, PartitionSpec as P

HEAD = 64
BF = jnp.bfloat16
F32 = jnp.float32
REP = ("x", "core")
SHARD = ("z", "y")
NEG = -1e30
GATHER_ROUND = 2


def dot(left, right):
    return jnp.dot(left, right, preferred_element_type=F32)


def dot_nt(left, right):
    return lax.dot_general(left, right, (((1,), (1,)), ((), ())), preferred_element_type=F32)


def dot_tn(left, right):
    return lax.dot_general(left, right, (((0,), (0,)), ((), ())), preferred_element_type=F32)


def iota(shape, dim):
    return lax.broadcasted_iota(jnp.int32, shape, dim)


def doc_starts(places, ends_ref):
    starts = jnp.zeros_like(places)
    for n in range(ends_ref.shape[0]):
        starts = jnp.where(places >= ends_ref[n], ends_ref[n], starts)
    return starts


def first_block(block, tile, ends_ref):
    row = block * tile
    start = jnp.int32(0)
    for n in range(ends_ref.shape[0]):
        start = jnp.where(row >= ends_ref[n], ends_ref[n], start)
    return lax.div(start, jnp.int32(tile))


def rows(block, tile):
    return pl.ds(pl.multiple_of(block * tile, tile), tile)


def only_head(values, head):
    lanes = iota(values.shape, 1)
    keep = (lanes < HEAD) if head == 0 else (lanes >= HEAD)
    return jnp.where(keep, values, jnp.zeros_like(values))


def tail_slots(tail):
    lanes = iota(tail.shape, 1)
    spare = tail.shape[1] // 2
    weight = jnp.where(lanes == spare, 64.0, jnp.where(lanes == spare + 1, 1.0, 0.0))
    return tail.astype(F32) * weight


def forward_kernel(blocks, ends_ref, spot_ref, *refs):
    h_refs, refs = refs[:blocks], refs[blocks:]
    (
        wa_ref, wb_ref, bias_ref, own_ref,
        sp_ref, kt_ref, o_ref, of_ref, lse_ref, q16_ref, o16_ref, lse16_ref, w_ref, srow_ref, scol_ref,
        p_scr, vt_scr, ob_scr, row_scr,
    ) = refs
    tile = own_ref.shape[1]
    total = blocks * tile
    feats = wa_ref.shape[1]
    wide = in_width(feats, blocks)
    z, y, corner = spot_ref[0], spot_ref[1], spot_ref[2]
    zs = blocks // 2

    w_ref[...] = jnp.zeros_like(w_ref)
    for c in range(4):
        @pl.when(corner == c)
        def _(c=c):
            for n, (ref, at) in enumerate(((wa_ref, 0), (wa_ref, 1), (wb_ref, 0), (wb_ref, 1))):
                place = c ^ n
                w_ref[:feats, place * wide:(place + 1) * wide] = ref[at, :, :wide]

    me = z * 2 + y
    lanes = pl.ds(pl.multiple_of(me * 128, 128), 128)
    blank = jnp.zeros((1, 128), F32)
    last = bias_ref.shape[1] - HEAD
    bias = jnp.concatenate(
        [
            bias_ref[1:2, lanes], blank, bias_ref[2:3, lanes],
            blank[:, :HEAD], bias_ref[2:3, last:], bias_ref[1:2, last:], blank[:, :HEAD],
        ],
        axis=1,
    )
    for b in range(blocks):
        r = slice(b * tile, (b + 1) * tile)
        p_scr[r, :] = (dot(h_refs[b][...], w_ref[...]) + bias).astype(BF)
        tail = tail_slots(h_refs[b][:, h_refs[b].shape[1] - 128:])
        scol_ref[r, :] = jnp.sum(tail, axis=1, keepdims=True).astype(jnp.int32)
        row = jnp.sum(tail.T, axis=0, keepdims=True).astype(jnp.int32)
        row_scr[:, r] = row
        shard = lax.rem(z + zs - b // 2, zs) * 2 + lax.rem(y + b % 2, 2)
        srow_ref[shard] = row

    @pl.loop(0, blocks)
    def _(b):
        r = rows(b, tile)
        place = iota((tile, total), 0) + b * tile
        pick = jnp.where(row_scr[...] == place, 1.0, 0.0).astype(BF)
        sorted_f = dot(pick, p_scr[:, :512])
        sp_ref[r, :] = sorted_f.astype(BF)
        kt_ref[b] = sorted_f[:, 128:256].T.astype(BF)
        vt_scr[b, :128, :] = sorted_f[:, 256:384].T.astype(BF)
        vt_scr[b, 128:, :] = sorted_f[:, 384:512].T.astype(BF)

    q16 = p_scr[0:tile, 512:640]
    q16_ref[...] = q16

    @pl.loop(0, blocks)
    def _(qb):
        q = sp_ref[rows(qb, tile), 0:128]
        qs = [only_head(q, 0), only_head(q, 1)]
        qpos = iota((1, tile), 1) + qb * tile
        qstart = doc_starts(qpos, ends_ref)
        low = first_block(qb, tile, ends_ref)

        def step(n, state):
            kb = qb - n
            k = sp_ref[rows(kb, tile), 128:256]
            kpos = iota((tile, tile), 0) + kb * tile
            ok = (kpos <= qpos) & (kpos >= qstart)
            new = []
            for head in range(2):
                m, l, acc = state[head]
                s = jnp.where(ok, dot_nt(k, qs[head]) * 0.125, NEG)
                mn = jnp.maximum(m, jnp.max(s, axis=0, keepdims=True))
                p = jnp.exp(s - mn)
                a = jnp.exp(m - mn)
                l = l * a + jnp.sum(p, axis=0, keepdims=True)
                vt = vt_scr[kb, head * HEAD:(head + 1) * HEAD, :]
                acc = acc * a + dot(vt, p.astype(BF))
                new.append((mn, l, acc))
            return tuple(new)

        start = (jnp.full((1, tile), NEG, F32), jnp.zeros((1, tile), F32), jnp.zeros((HEAD, tile), F32))
        state = lax.fori_loop(0, qb - low + 1, step, (start, start))
        out = jnp.concatenate([state[0][2] / state[0][1], state[1][2] / state[1][1]], axis=0).T
        of_ref[rows(qb, tile), :] = out
        ob_scr[rows(qb, tile), :] = out.astype(BF)
        lse_ref[qb] = jnp.concatenate([s[0] + jnp.log(s[1]) for s in state], axis=0)

    own = own_ref[...]
    own_start = doc_starts(own, ends_ref)

    def step16(kb, state):
        m, l, acc = state
        kv = sp_ref[rows(kb, tile), 384:512]
        kpos = iota((tile, tile), 0) + kb * tile
        ok = (kpos <= own) & (kpos >= own_start)
        s = jnp.where(ok, dot_nt(kv, q16) * 0.125, NEG)
        mn = jnp.maximum(m, jnp.max(s, axis=0, keepdims=True))
        p = jnp.where(ok, jnp.exp(s - mn), 0.0)
        a = jnp.exp(m - mn)
        l = l * a + jnp.sum(p, axis=0, keepdims=True)
        acc = acc * a + dot(vt_scr[kb, 192:256, :], p.astype(BF))
        return mn, l, acc

    start = (jnp.full((1, tile), NEG, F32), jnp.zeros((1, tile), F32), jnp.zeros((HEAD, tile), F32))
    m, l, acc = lax.fori_loop(0, blocks, step16, start)
    o16_ref[...] = jnp.concatenate([jnp.zeros_like(acc), acc / l], axis=0).T
    lse16_ref[...] = m + jnp.log(l)

    for b in range(blocks):
        pick = jnp.where(scol_ref[b * tile:(b + 1) * tile, :] == iota((tile, total), 1), 1.0, 0.0).astype(BF)
        shard = lax.rem(z + zs - b // 2, zs) * 2 + lax.rem(y + b % 2, 2)
        o_ref[shard] = dot(pick, ob_scr[...]).astype(BF)


def backward_kernel(
    ends_ref, w_ref, srow_ref, scol_ref, own_ref, sp_ref, kt_ref, of_ref, lse_ref,
    do_ref, q16_ref, do16_ref, o16_ref, lse16_ref,
    dp_ref, dq16_ref, *refs,
):
    total = sp_ref.shape[0]
    tile = own_ref.shape[1]
    blocks = total // tile
    dh_refs, (dos_scr, acc_scr, acc16_scr, dps_scr) = refs[:blocks], refs[blocks:]

    places = jnp.concatenate([srow_ref[b] for b in range(blocks)], axis=1)

    @pl.loop(0, blocks)
    def _(b):
        r = rows(b, tile)
        pick = jnp.where(places == iota((tile, total), 0) + b * tile, 1.0, 0.0).astype(BF)
        dos_scr[r, :] = dot(pick, do_ref[...]).astype(BF)
        acc_scr[r, :] = jnp.zeros((tile, 256), F32)

    @pl.loop(0, blocks)
    def _(qb):
        qr = rows(qb, tile)
        q = sp_ref[qr, 0:128]
        do = dos_scr[qr, :]
        qs = [only_head(q, 0), only_head(q, 1)]
        ds_ = [only_head(do, 0), only_head(do, 1)]
        q_two = jnp.concatenate(qs, axis=0)
        do_two = jnp.concatenate(ds_, axis=0)
        prod = (do.astype(F32) * of_ref[qr, :]).T
        delta = [jnp.sum(prod[:HEAD], axis=0, keepdims=True), jnp.sum(prod[HEAD:], axis=0, keepdims=True)]
        lse = lse_ref[qb]
        qpos = iota((1, tile), 1) + qb * tile
        qstart = doc_starts(qpos, ends_ref)
        low = first_block(qb, tile, ends_ref)

        def step(kb, dqt):
            kr = rows(kb, tile)
            k = sp_ref[kr, 128:256]
            v = sp_ref[kr, 256:384]
            kpos = iota((tile, tile), 0) + kb * tile
            ok = (kpos <= qpos) & (kpos >= qstart)
            ps, dss, new = [], [], []
            for head in range(2):
                s = dot_nt(k, qs[head]) * 0.125 - lse[head:head + 1]
                p = jnp.where(ok, jnp.exp(s), 0.0)
                dprob = dot_nt(v, ds_[head])
                ds = (p * (dprob - delta[head])).astype(BF)
                ps.append(p.astype(BF))
                dss.append(ds)
                new.append(dqt[head] + dot(kt_ref[kb, head * HEAD:(head + 1) * HEAD, :], ds))
            acc_scr[kr, 0:128] += dot(jnp.concatenate(dss, axis=1), q_two)
            acc_scr[kr, 128:256] += dot(jnp.concatenate(ps, axis=1), do_two)
            return tuple(new)

        zero = jnp.zeros((HEAD, tile), F32)
        dqt = lax.fori_loop(low, qb + 1, step, (zero, zero))
        dps_scr[qr, 0:128] = (jnp.concatenate(dqt, axis=0).T * 0.125).astype(BF)

    own = own_ref[...]
    own_start = doc_starts(own, ends_ref)
    q16 = q16_ref[...]
    do16 = do16_ref[...]
    both = jnp.concatenate([q16, do16], axis=0)
    delta16 = jnp.sum((do16.astype(F32) * o16_ref[...]).T, axis=0, keepdims=True)
    lse16 = lse16_ref[...]

    def step16(kb, dq):
        kr = rows(kb, tile)
        kv = sp_ref[kr, 384:512]
        kpos = iota((tile, tile), 0) + kb * tile
        ok = (kpos <= own) & (kpos >= own_start)
        p = jnp.where(ok, jnp.exp(dot_nt(kv, q16) * 0.125 - lse16), 0.0)
        ds = (p * (dot_nt(kv, do16) - delta16)).astype(BF)
        acc16_scr[kr, :] = dot(jnp.concatenate([ds, p.astype(BF)], axis=1), both)
        return dq + dot_tn(ds, kv)

    dq16 = lax.fori_loop(0, blocks, step16, jnp.zeros((tile, 128), F32))
    dq16 = (dq16 * 0.125).astype(BF)
    dq16_ref[...] = dq16

    @pl.loop(0, blocks)
    def _(b):
        r = rows(b, tile)
        dps_scr[r, 128:256] = (acc_scr[r, 0:128] * 0.125).astype(BF)
        dps_scr[r, 256:384] = acc_scr[r, 128:256].astype(BF)
        part = acc16_scr[r, :]
        dps_scr[r, 384:512] = jnp.where(iota(part.shape, 1) < HEAD, part * 0.125, part).astype(BF)

    for b in range(blocks):
        r = slice(b * tile, (b + 1) * tile)
        pick = jnp.where(scol_ref[r, :] == iota((tile, total), 1), 1.0, 0.0).astype(BF)
        dp = dot(pick, dps_scr[...]).astype(BF)
        dp_ref[r, :] = dp
        dh = dot_nt(dp, w_ref[:, :512])
        if b == 0:
            dh = dh + dot_nt(only_head(dq16, 0), w_ref[:, 512:640])
        dh_refs[b][...] = dh[:, :dh_refs[b].shape[1]].astype(BF)


def norm_stats(values):
    centre = values - jnp.mean(values, axis=-1, keepdims=True)
    spread = jnp.mean(centre * centre, axis=-1, keepdims=True)
    rate = lax.rsqrt(spread + 1e-05)
    return centre * rate, rate


def norm_back(grad, normed, rate, gain):
    scaled = grad * gain
    inner = jnp.mean(scaled * normed, axis=-1, keepdims=True)
    back = rate * (scaled - jnp.mean(scaled, axis=-1, keepdims=True) - normed * inner)
    return back, jnp.sum(grad * normed, axis=0, keepdims=True), jnp.sum(grad, axis=0, keepdims=True)


def put(ref, values):
    width = values.shape[1]
    ref[:, :width] = values
    ref[:, width:] = jnp.zeros((ref.shape[0], ref.shape[1] - width), ref.dtype)


def first_norm_kernel(tok_ref, slot_ref, gain_ref, bias_ref, h_ref):
    tile, feats = tok_ref.shape
    normed, _ = norm_stats(tok_ref[...].astype(F32))
    h_ref[:, :feats] = (normed * gain_ref[0:1] + bias_ref[0:1]).astype(BF)
    width = h_ref.shape[1] - feats
    slot = slot_ref[...]
    high = lax.shift_right_logical(slot, 6)
    lanes = iota((tile, width), 1)
    pair = jnp.where(lanes == 0, high, jnp.where(lanes == 1, slot - high * 64, 0))
    h_ref[:, feats:] = pair.astype(F32).astype(BF)


def slab(feats, n_shard, shard):
    mine = feats // HEAD // n_shard * HEAD
    spare = n_shard * mine
    left = feats - spare
    return [
        (shard * mine, mine), (feats + shard * mine, mine), (2 * feats + shard * mine, mine),
        (feats + spare, left), (2 * feats + spare, left), (spare, left),
    ]


def slab_part(feats, n_shard, shard, low, high):
    found, at = [], 0
    for start, width in slab(feats, n_shard, shard):
        first, end = max(at, low), min(at + width, high)
        if first < end:
            found.append((start + first - at, end - first, first - low))
        at = at + width
    return found


def in_width(feats, n_shard):
    return sum(width for _, width in slab(feats, n_shard, 0)) // 4


def pack_in_kernel(spot_ref, w_ref, out_w_ref, out_ref):
    feats = w_ref.shape[1] // 3
    n_shard = out_ref.shape[0]
    wide, out_wide = in_width(feats, n_shard), feats // 4
    for c in range(4):
        @pl.when(spot_ref[2] == c)
        def _(c=c):
            for s in range(n_shard):
                for column, width, place in slab_part(feats, n_shard, s, c * wide, (c + 1) * wide):
                    out_ref[s, :, place:place + width] = w_ref[:, column:column + width]
                out_ref[s, :, wide:wide + out_wide] = out_w_ref[:, c * out_wide:(c + 1) * out_wide]
                out_ref[s, :, wide + out_wide:] = jnp.zeros_like(out_ref[s, :, wide + out_wide:])


def pack_ff_kernel(n_shard, spot_ref, up_ref, down_ref, bias_ref, out_ref, own_bias_ref):
    feats = down_ref.shape[1]
    quarter = down_ref.shape[0] // 4
    aligned = -(-feats // 128) * 128
    out_ref[...] = jnp.zeros_like(out_ref)
    for c in range(4):
        r = (c % 2) * 2 + c // 2

        @pl.when(spot_ref[2] == c)
        def _(c=c, r=r):
            for s in range(n_shard):
                at = (s * 4 + r) * quarter
                out_ref[:, s * quarter:(s + 1) * quarter] = up_ref[:, at:at + quarter]
                own_bias_ref[:, s * quarter:(s + 1) * quarter] = bias_ref[:, at:at + quarter]
            out_ref[:, aligned:aligned + feats] = down_ref[r * quarter:(r + 1) * quarter, :]


def middle_kernel(
    spot_ref, o_ref, o16_ref, wa_ref, wb_ref, tok_ref, gain_ref, bias_ref,
    h_ref, middle_ref, attended_ref, w_ref,
):
    n_shard, tile, mine = o_ref.shape
    feats = tok_ref.shape[1]
    wide, first = feats // 4, in_width(feats, n_shard)
    for s in range(n_shard):
        attended_ref[:, s * mine:(s + 1) * mine] = o_ref[s]
    attended_ref[:, n_shard * mine:] = o16_ref[:, HEAD:].astype(BF)
    for c in range(4):
        @pl.when(spot_ref[2] == c)
        def _(c=c):
            for n, (ref, at) in enumerate(((wa_ref, 0), (wa_ref, 1), (wb_ref, 0), (wb_ref, 1))):
                place = c ^ n
                w_ref[:, place * wide:(place + 1) * wide] = ref[at, :, first:first + wide]
    middle = tok_ref[...].astype(F32) + (dot(attended_ref[...], w_ref[...]) + bias_ref[3:4])
    middle_ref[...] = middle
    normed, _ = norm_stats(middle)
    put(h_ref, (normed * gain_ref[1:2] + bias_ref[4:5]).astype(BF))


def by_corner(spot_ref, full_ref, wide, keep_a, keep_b, send_ref):
    for c in range(4):
        @pl.when(spot_ref[2] == c)
        def _(c=c):
            for n in range(4):
                p = c ^ n
                part = full_ref[:, p * wide:(p + 1) * wide]
                if n < 2:
                    put((keep_a, keep_b)[n], part)
                else:
                    put(send_ref.at[n - 2], part.astype(BF))


def middle_back_kernel(
    spot_ref, kept_ref, core_ref, far_ref, middle_ref, w_ref, cot_ref, attended_ref, gain_ref,
    dmiddle_ref, do_ref, do16_ref, keep_a, keep_b, send_ref, sums_ref, full_scr,
):
    n_shard, tile, mine = do_ref.shape
    feats = middle_ref.shape[1]
    dh = (kept_ref[...] + core_ref[...].astype(F32) + far_ref[...].astype(F32))[:, :feats]
    normed, rate = norm_stats(middle_ref[...])
    dout = cot_ref[:, :feats].astype(F32)
    back, gain_sum, bias_sum = norm_back(dh, normed, rate, gain_ref[1:2])
    dmiddle = dout + back
    dmiddle_ref[...] = dmiddle
    dbranch = dmiddle.astype(BF)
    dattended = dot_nt(dbranch, w_ref[...]).astype(BF)
    for s in range(n_shard):
        do_ref[s] = dattended[:, s * mine:(s + 1) * mine]
    last = dattended[:, n_shard * mine:]
    do16_ref[...] = jnp.concatenate([jnp.zeros_like(last), last], axis=1)
    full_scr[...] = dot_tn(attended_ref[...], dbranch)
    by_corner(spot_ref, full_scr, feats // 4, keep_a, keep_b, send_ref)
    sums_ref[0:1] = jnp.sum(dbranch.astype(F32), axis=0, keepdims=True)
    sums_ref[1:2] = bias_sum
    sums_ref[2:3] = jnp.sum(dout, axis=0, keepdims=True)
    sums_ref[3:4] = gain_sum


def last_kernel(kept_ref, y_ref, a_ref, b_ref, dmiddle_ref, tok_ref, gain_ref, out_ref, sums_ref):
    dh = kept_ref[...].astype(F32) + y_ref[...].astype(F32) + a_ref[...].astype(F32) + b_ref[...].astype(F32)
    dh = dh[:, :tok_ref.shape[1]]
    normed, rate = norm_stats(tok_ref[...].astype(F32))
    back, gain_sum, bias_sum = norm_back(dh, normed, rate, gain_ref[0:1])
    out_ref[...] = dmiddle_ref[...] + back
    sums_ref[0:1] = bias_sum
    sums_ref[1:2] = gain_sum


def feed_forward_kernel(
    h_a, h_b, h_c, g_a, g_b, g_c, w_ref, bias_ref,
    act_ref, dpre_ref, keep_a, keep_b, send_ref, sum_ref,
):
    tile, aligned = h_a.shape
    units, feats = act_ref.shape[1], w_ref.shape[0]
    total = jnp.zeros((1, units), F32)
    sources = ((h_a, g_a, None), (h_b, g_b, None), (h_c, g_c, 0), (h_c, g_c, 1))
    for n, (h_ref, g_ref, at) in enumerate(sources):
        h = h_ref[:, :feats] if at is None else h_ref[at, :, :feats]
        g = g_ref[:, :feats] if at is None else g_ref[at, :, :feats]
        r = slice(n * tile, (n + 1) * tile)
        pre = dot(h, w_ref[:, :units]) + bias_ref[...]
        dact = dot_nt(g, w_ref[:, aligned:aligned + feats])
        square = pre * pre
        root = 0.7978845608028654
        flat = jnp.tanh(root * pre * (1.0 + 0.044715 * square))
        half = 0.5 * (1.0 + flat)
        act_ref[r, :] = (pre * half).astype(BF)
        slope = half + 0.5 * pre * (1.0 - flat * flat) * root * (1.0 + 0.134145 * square)
        dpre = (dact * slope).astype(BF)
        dpre_ref[r, :] = dpre
        total = total + jnp.sum(dpre.astype(F32), axis=0, keepdims=True)
        dh = dot_nt(dpre, w_ref[:, :units])
        if n < 2:
            put((keep_a, keep_b)[n], dh)
        else:
            put(send_ref.at[n - 2], dh.astype(BF))
    sum_ref[...] = total


def feed_grads_kernel(
    h_a, h_b, h_c, g_a, g_b, g_c, w_ref, act_ref, dpre_ref,
    keep_a, keep_b, send_ref, grad_ref, h_scr, g_scr,
):
    tile, aligned = h_a.shape
    units, feats = act_ref.shape[1], w_ref.shape[0]
    down = w_ref[:, aligned:aligned + feats]
    sources = ((h_a, g_a, None), (h_b, g_b, None), (h_c, g_c, 0), (h_c, g_c, 1))
    for n, (h_ref, g_ref, at) in enumerate(sources):
        r = slice(n * tile, (n + 1) * tile)
        h_scr[r, :] = h_ref[:, :feats] if at is None else h_ref[at, :, :feats]
        g_scr[r, :] = g_ref[:, :feats] if at is None else g_ref[at, :, :feats]
    step = 256
    for at in range(0, units, step):
        c = slice(at, min(at + step, units))
        grad_ref[:, c] = dot_tn(h_scr[...], dpre_ref[:, c]).astype(BF)
    for at in range(0, feats, step):
        end = min(at + step, feats)
        part = dot_tn(act_ref[...], g_scr[:, at:end])
        grad_ref[:, aligned + at:aligned + end] = part.astype(BF)
    blank = jnp.zeros((grad_ref.shape[0], aligned - feats), BF)
    grad_ref[:, units:aligned] = blank
    grad_ref[:, aligned + feats:2 * aligned] = blank
    for n in range(4):
        mixed = dot(act_ref[n * tile:(n + 1) * tile, :], down)
        if n < 2:
            put((keep_a, keep_b)[n], mixed)
        else:
            put(send_ref.at[n - 2], mixed.astype(BF))


def in_grad_kernel(blocks, spot_ref, *refs):
    h_refs, (dp_ref, dq16_ref, keep_a, keep_b, send_ref, full_scr) = refs[:blocks], refs[blocks:]
    tile = dq16_ref.shape[0]
    feats = keep_a.shape[0]
    for at in range(0, 512, 256):
        acc = dot_tn(h_refs[0][:, :feats], dp_ref[:tile, at:at + 256])
        for b in range(1, blocks):
            acc = acc + dot_tn(h_refs[b][:, :feats], dp_ref[b * tile:(b + 1) * tile, at:at + 256])
        full_scr[:, at:at + 256] = acc
    full_scr[:, 512:576] = dot_tn(h_refs[0][:, :feats], dq16_ref[...])[:, :HEAD]
    by_corner(spot_ref, full_scr, in_width(feats, blocks), keep_a, keep_b, send_ref)


def fold_kernel(wide, in_ref, out_ref):
    for s in range(in_ref.shape[0]):
        out_ref[:, s * wide:(s + 1) * wide] = in_ref[s, :, :wide]


def fill_kernel(all_ref, a_ref, b_ref, c_ref, out_ref):
    out_ref[...] = (a_ref[...] + b_ref[...].astype(F32) + c_ref[...].astype(F32)).astype(BF)


def filled(values, terms):
    count, wide = terms[0].shape
    last = values.shape[1] // wide - 1
    part = pl.BlockSpec((count, wide), lambda n: (0, 0))
    return pl.pallas_call(
        fill_kernel,
        grid=(1,),
        out_shape=jax.ShapeDtypeStruct(values.shape, values.dtype),
        in_specs=[pl.BlockSpec(memory_space=pl.ANY)] + [part] * 3,
        out_specs=pl.BlockSpec((count, wide), lambda n: (0, last)),
        input_output_aliases={0: 0},
        compiler_params=pltpu.CompilerParams(vmem_limit_bytes=32 * 2**20),
    )(values, *terms)


def owned_kernel(n_shard, spot_ref, a_ref, b_ref, c_ref, up_ref, down_ref, out_w_ref):
    quarter, feats = a_ref.shape[0], down_ref.shape[1]
    aligned = -(-feats // 128) * 128
    out_wide = feats // 4
    for c in range(4):
        @pl.when(spot_ref[2] == c)
        def _(c=c):
            for n, (ref, at) in enumerate(((a_ref, None), (b_ref, None), (c_ref, 0), (c_ref, 1))):
                place = c ^ n
                r = (place % 2) * 2 + place // 2
                part = ref[...] if at is None else ref[at]
                for s in range(n_shard):
                    to = (s * 4 + r) * quarter
                    up_ref[:, to:to + quarter] = part[:, s * quarter:(s + 1) * quarter].astype(F32)
                down_ref[r * quarter:(r + 1) * quarter, :] = part[:, aligned:aligned + feats].astype(F32)
                out_part = part[:, 2 * aligned:2 * aligned + out_wide].astype(F32)
                out_w_ref[:, place * out_wide:(place + 1) * out_wide] = out_part


def owned_in_kernel(n_shard, spot_ref, a_ref, b_ref, c_ref, out_ref):
    feats = out_ref.shape[1] // 3
    wide = in_width(feats, n_shard)
    shared = 3 * (feats // HEAD // n_shard * HEAD)
    for c in range(4):
        @pl.when(spot_ref[2] == c)
        def _(c=c):
            for n, (ref, at) in enumerate(((a_ref, None), (b_ref, None), (c_ref, 0), (c_ref, 1))):
                place = c ^ n
                low = place * wide

                def block(s):
                    lanes = slice(s * wide, (s + 1) * wide)
                    return (ref[:, lanes] if at is None else ref[at, :, lanes]).astype(F32)

                for s in range(n_shard):
                    for column, width, to in slab_part(feats, n_shard, s, low, min(low + wide, shared)):
                        out_ref[:, column:column + width] = block(s)[:, to:to + width]
                if low + wide > shared:
                    total = block(0)
                    for s in range(1, n_shard):
                        total = total + block(s)
                    first = max(low, shared)
                    for column, width, to in slab_part(feats, n_shard, 0, first, low + wide):
                        to = to + first - low
                        out_ref[:, column:column + width] = total[:, to:to + width]


VM = pl.BlockSpec(memory_space=pltpu.VMEM)
SM = pl.BlockSpec(memory_space=pltpu.SMEM)


def run(kernel, outs, operands, scalars=0, scratch=(), size=58, flops=0.0):
    moved = sum(v.size * v.dtype.itemsize for v in operands)
    moved = moved + sum(math.prod(shape) * jnp.dtype(kind).itemsize for shape, kind in outs)
    return pl.pallas_call(
        kernel,
        out_shape=tuple(jax.ShapeDtypeStruct(shape, kind) for shape, kind in outs),
        in_specs=[SM] * scalars + [VM] * (len(operands) - scalars),
        out_specs=tuple([VM] * len(outs)),
        scratch_shapes=[pltpu.VMEM(shape, kind) for shape, kind in scratch],
        compiler_params=pltpu.CompilerParams(vmem_limit_bytes=size * 2**20),
        cost_estimate=pl.CostEstimate(flops=int(flops), bytes_accessed=int(moved), transcendentals=0),
    )(*operands)


def swap(values, axis):
    return lax.ppermute(values, axis, [(0, 1), (1, 0)])


def gather_rep(values):
    other = swap(values, "x")
    return values, other, swap(jnp.stack([values, other]), "core")


def scatter_rep(keep_a, keep_b, send):
    across = swap(send, "core")
    return keep_a, across[0], swap((keep_b + across[1].astype(F32)).astype(BF), "x")


def shift(values, step):
    size = lax.axis_size("z")
    return lax.ppermute(values, "z", [(n, (n + step) % size) for n in range(size)])


def together(*values):
    return lax.optimization_barrier(values)


def ring_gather(values, beside):
    size = lax.axis_size("z")
    column = [values] + [None] * (size - 1)
    other = [None] * size
    arrived, last = [(0, values)], {1: values, -1: values}
    for n in range(1, size // 2 + 2):
        places, moving = [], []
        for place, block in arrived:
            places.append((other, place))
            moving.append(swap(block, "y"))
        arrived = []
        if n <= size // 2:
            steps = (1, -1) if size - n > n else (1,)
            for step in steps:
                places.append((column, n if step == 1 else size - n))
                moving.append(shift(last[step], step))
        moving = beside(n, moving)
        for (target, place), block in zip(places, moving):
            target[place] = block
            if target is column:
                arrived.append((place, block))
                last[1 if place == n else -1] = block
    return [block for pair in zip(column, other) for block in pair]


def ring_scatter(parts, beside):
    size = lax.axis_size("z")
    kept, sent = parts[0::2], parts[1::2]
    half = size // 2
    joined, running = {}, {1: None, -1: None}
    wanted = [[half] + ([size - half + 1] if size - half + 1 < size else [])]
    wanted += [[n] + ([size - n + 1] if size - n + 1 < size else []) for n in range(half - 1, 0, -1)]
    wanted += [[0]]
    for index, now in enumerate(wanted + [[]]):
        moving = [swap(sent[n], "y") for n in now]
        steps = []
        if index > 0:
            n = half + 1 - index
            for step, place in ((-1, n), (1, size - n)):
                if n >= 1 and (step == -1 or size - n > n):
                    total = joined[place]
                    if running[step] is not None:
                        total = total + running[step].astype(F32)
                    steps.append(step)
                    moving.append(shift(total.astype(BF), step))
        if not moving:
            continue
        moving = beside(index + 1, moving)
        for n, block in zip(now, moving):
            joined[n] = block if n == 0 else kept[n].astype(F32) + block.astype(F32)
        for step, block in zip(steps, moving[len(now):]):
            running[step] = block
    return kept[0], joined[0], running[-1], running[1]


def sum_dp(values):
    if lax.axis_size("dp") > 1:
        return lax.psum(values, "dp")
    return values


def sum_all(values):
    z_size = lax.axis_size("z")
    for axis in ("core", "x", "y"):
        values = values + swap(values, axis)
    step = 1
    while step < z_size:
        values = values + lax.ppermute(values, "z", [(n, n ^ step) for n in range(z_size)])
        step = step * 2
    return sum_dp(values)


def gather_shard(values):
    return lax.all_gather(values, SHARD, axis=0, tiled=True)


def scatter_shard(values):
    return lax.psum_scatter(values.astype(BF), SHARD, scatter_dimension=0, tiled=True)


def exchange_shard(values):
    return lax.all_to_all(values, SHARD, 0, 0, tiled=True)


def shards(
    tokens, slot, lengths, attn_in_weight, attn_out_weight, up_weight, down_weight,
    norm_gains, layer_biases, up_bias, cotangent,
):
    tile, feats = tokens.shape
    zs = lax.axis_size("z")
    n_shard = zs * 2
    total = n_shard * tile
    mine = feats // HEAD // n_shard * HEAD
    spare = n_shard * mine
    z, y = lax.axis_index("z"), lax.axis_index("y")
    me = z * 2 + y
    rep = lax.axis_index("x") * 2 + lax.axis_index("core")
    corner = lax.axis_index("core") * 2 + lax.axis_index("x")
    spot = jnp.stack([z, y, corner]).astype(jnp.int32)
    row_part = attn_in_weight.shape[0]
    ff_part = down_weight.shape[0]
    n_rep = 4
    quarter = ff_part // n_rep
    units = n_shard * quarter
    aligned = -(-feats // 128) * 128
    in_wide = in_width(feats, n_shard)
    out_wide = feats // n_rep
    both_wide = -(-(in_wide + out_wide) // 128) * 128
    in_full = -(-in_wide // 128) * 128
    out_full = -(-out_wide // 128) * 128
    fold_wide = -(-(n_shard * in_wide) // 128) * 128

    ends = jnp.cumsum(lengths[0]).astype(jnp.int32)
    (h_first,) = run(
        first_norm_kernel, [((tile, aligned), BF)], (tokens, slot.reshape(tile, 1), norm_gains, layer_biases)
    )

    (in_pack,) = run(
        pack_in_kernel, [((n_shard, row_part, both_wide), BF)], (spot, attn_in_weight, attn_out_weight), 1
    )
    ff_pack, up_bias_mine = run(
        functools.partial(pack_ff_kernel, n_shard),
        [((row_part, 2 * aligned), BF), ((1, units), F32)],
        (spot, up_weight, down_weight, up_bias.reshape(1, -1)), 1,
    )
    held = dict(
        in_own=exchange_shard(in_pack).reshape(feats, both_wide),
        dout=jnp.pad(cotangent, ((0, 0), (0, aligned - feats))),
        ff_pack=ff_pack,
    )

    def beside_gather(n, moving):
        names = []
        if n == 1:
            names = ["in_own", "dout", "ff_pack"]
        elif n == 2:
            held["in_far"], held["dout_far"] = swap(held["in_own"], "x"), swap(held["dout"], "x")
            names = ["in_own", "in_far", "dout", "dout_far", "ff_pack"]
        elif n == 3:
            held["in_a"] = jnp.stack([held["in_own"], held["in_far"]])
            held["in_b"] = swap(held["in_a"], "core")
            held["g_core"] = swap(jnp.stack([held["dout"], held["dout_far"]]), "core")
            names = ["in_a", "in_b", "dout", "dout_far", "g_core"]
        *moving, = together(*moving, *[held[name] for name in names])
        for name in reversed(names):
            held[name] = moving.pop()
        if n == GATHER_ROUND:
            held["w_all"] = gather_shard(held["ff_pack"])
        return moving

    h_parts = ring_gather(h_first, beside_gather)
    w_all, in_a, in_b = held["w_all"], held["in_a"], held["in_b"]
    dout, g_rep = held["dout"], (held["dout"], held["dout_far"], held["g_core"])
    (sp, kt, o_own, of, lse, q16, o16, lse16, w_own, slot_rows, slot_columns) = run(
        functools.partial(forward_kernel, n_shard),
        [
            ((total, 512), BF), ((n_shard, 128, tile), BF), ((n_shard, tile, 128), BF), ((total, 128), F32),
            ((n_shard, 2, tile), F32), ((tile, 128), BF), ((tile, 128), F32), ((1, tile), F32),
            ((aligned, 640), BF), ((n_shard, 1, tile), jnp.int32), ((total, 1), jnp.int32),
        ],
        (ends, spot, *h_parts, in_a, in_b, layer_biases, slot.reshape(1, tile)), 2,
        scratch=[((total, 640), BF), ((n_shard, 256, tile), BF), ((total, 128), BF), ((1, total), jnp.int32)],
        size=58, flops=30e9,
    )
    o_back = exchange_shard(o_own)
    h_second, middle, attended, w_out = run(
        middle_kernel,
        [((tile, aligned), BF), ((tile, feats), F32), ((tile, feats), BF), ((feats, feats), BF)],
        (spot, o_back, o16, in_a, in_b, tokens, norm_gains, layer_biases), 1, flops=2e9,
    )

    h_rep = gather_rep(h_second)
    whole, one, pair = (n_rep * tile, units), (tile, aligned), (2, tile, aligned)
    act, dpre, *dh_terms, up_bias_grad = run(
        feed_forward_kernel,
        [(whole, BF), (whole, BF), (one, F32), (one, F32), (pair, BF), ((1, units), F32)],
        (*h_rep, *g_rep, w_all, up_bias_mine), flops=10e9,
    )
    kept, joined, send = dh_terms
    across = swap(send, "core")
    joined, act, dpre = together((joined + across[1].astype(F32)).astype(BF), act, dpre)
    *mixed_terms, ff_grads = run(
        feed_grads_kernel,
        [(one, F32), (one, F32), (pair, BF), ((feats, 2 * aligned + out_full), BF)],
        (*h_rep, *g_rep, w_all, act, dpre),
        scratch=[((n_rep * tile, feats), BF)] * 2, size=58, flops=10e9,
    )
    far, ff_grads = together(swap(joined, "x"), ff_grads)
    dh_terms = (kept, across[0], far)
    mixed_terms = scatter_rep(*mixed_terms)
    mixed = (
        middle
        + (mixed_terms[0] + mixed_terms[1].astype(F32) + mixed_terms[2].astype(F32))[:, :feats]
        + layer_biases[5]
    ).astype(BF)

    dmiddle, do_all, do16, *out_terms, sums = run(
        middle_back_kernel,
        [
            ((tile, feats), F32), ((n_shard, tile, mine), BF), ((tile, 128), BF),
            ((feats, out_full), F32), ((feats, out_full), F32), ((2, feats, out_full), BF), ((4, feats), F32),
        ],
        (spot, *dh_terms, middle, w_out, dout, attended, norm_gains), 1,
        scratch=[((feats, feats), F32)], flops=3e9,
    )

    ff_grads = filled(ff_grads, scatter_rep(*out_terms))
    do_own, ff_grads = together(exchange_shard(do_all).reshape(total, mine), ff_grads)
    ff_owned = sum_dp(scatter_shard(ff_grads))
    dp, dq16, *dh_parts = run(
        backward_kernel,
        [((total, 512), BF), ((tile, 128), BF)] + [((tile, aligned), BF)] * n_shard,
        (
            ends, w_own, slot_rows, slot_columns, slot.reshape(1, tile),
            sp, kt, of, lse, do_own, q16, do16, o16, lse16,
        ),
        1,
        scratch=[((total, 128), BF), ((total, 256), F32), ((total, 128), F32), ((total, 512), BF)],
        size=58, flops=30e9,
    )
    in_kept, in_joined, in_send = run(
        functools.partial(in_grad_kernel, n_shard),
        [((feats, in_full), F32), ((feats, in_full), F32), ((2, feats, in_full), BF)],
        (spot, *h_parts, dp, dq16), 1, scratch=[((feats, 576), F32)], flops=3e9,
    )

    def beside_scatter(n, moving):
        if n == 3:
            across = swap(in_send, "core")
            far = swap((in_joined + across[1].astype(F32)).astype(BF), "x")
            *moving, across, far, held["ff"] = together(*moving, across, far, ff_owned)
            grad = (in_kept + across[0].astype(F32) + far.astype(F32)).astype(BF)
            held["in_back"] = exchange_shard(grad.reshape(n_shard, row_part, in_full))
        return moving

    dh_first = ring_scatter(dh_parts, beside_scatter)
    (in_back,) = run(functools.partial(fold_kernel, in_wide), [((row_part, fold_wide), BF)], (held["in_back"],))
    in_back = gather_rep(sum_dp(in_back))

    tokens_grad, first_sums = run(
        last_kernel, [((tile, feats), F32), ((2, feats), F32)], (*dh_first, dmiddle, tokens, norm_gains)
    )

    up_out, down_out, out_out = run(
        functools.partial(owned_kernel, n_shard),
        [((row_part, up_weight.shape[1]), F32), ((ff_part, feats), F32), ((row_part, feats), F32)],
        (spot, *gather_rep(held["ff"])), 1,
    )
    (in_out,) = run(
        functools.partial(owned_in_kernel, n_shard), [((row_part, 3 * feats), F32)], (spot, *in_back), 1
    )
    zeros = functools.partial(jnp.zeros, dtype=F32)
    dp_sums = jnp.sum(dp.astype(F32), axis=0)
    query_sums = lax.dynamic_update_slice(zeros(feats), dp_sums[:mine], (me * mine,))
    query_sums = query_sums + jnp.pad(jnp.sum(dq16[:, :HEAD].astype(F32), axis=0), (spare, 0))
    value_sums = lax.dynamic_update_slice(zeros(feats), dp_sums[2 * mine : 3 * mine], (me * mine,))
    value_sums = value_sums + jnp.pad(dp_sums[3 * mine + HEAD : 3 * mine + 2 * HEAD], (spare, 0))
    place = (jnp.arange(n_rep) == rep)[:, None]
    vectors = jnp.concatenate(
        [
            first_sums[0:1], jnp.stack([query_sums, value_sums]), sums[0:3], first_sums[1:2], sums[3:4],
            jnp.where(place, up_bias_grad, 0.0),
        ]
    )
    vectors = lax.dynamic_slice_in_dim(sum_all(vectors), me * row_part, row_part, 1)
    return (
        mixed, tokens_grad, in_out, out_out, up_out, down_out,
        vectors[6:8], vectors[0:6], vectors[8:].reshape(-1),
    )


def solution(mesh):
    replicas, n_shard = mesh.shape["replica"], mesh.shape["shard"]
    fine = Mesh(
        mesh.devices.reshape(replicas // 4, 2, 2, n_shard // 2, 2), ("dp", "x", "core", "z", "y")
    )
    rep = ("dp", "x", "core")
    both = rep + SHARD
    in_specs = (
        P(both, None), P(both), P(rep, None), P(SHARD, None), P(SHARD, None), P(SHARD, None), P(SHARD, None),
        P(), P(), P(), P(both, None),
    )
    out_specs = (
        P(both, None), P(both, None), P(SHARD, None), P(SHARD, None), P(SHARD, None), P(SHARD, None),
        P(None, SHARD), P(None, SHARD), P(SHARD),
    )
    return jax.shard_map(shards, mesh=fine, in_specs=in_specs, out_specs=out_specs, check_vma=False)
```

time: 739 us -> 537 us (0.73)
  local copies, waits for them, and re-layouts: 148 us -> 25.6 us
  waiting for transfers between devices: 319 us -> 205 us
  Pallas kernels: 70 us -> 161 us
  matrix products: 56.7 us -> 0 us
  starting transfers between devices: 32 us -> 64.2 us
  other arithmetic: 39.1 us -> 22.9 us
  blocking collectives: 47.7 us -> 37.9 us
    reduce_scatter x2 -> x0, waiting for transfers between devices: 115 us -> none  [scatter_shard(): lax.psum_scatter(values.astype(BF), SHARD, scatter_dimension=0, tiled=True)]
    pallas_call x2 -> x15, Pallas kernels: 70 us -> 161 us  [the longest x14 161 us: run(): pl.pallas_call(kernel, out_shape=tuple((jax.ShapeDtypeStruct(shape, kind)...]
    ppermute x17 -> x29, waiting for transfers between devices: 63 us -> 150 us  [swap(): return lax.ppermute(values, axis, [(0, 1), (1, 0)])]
    all_gather x3 -> x1, waiting for transfers between devices: 81.1 us -> 0.01 us  [gather_shard(): return lax.all_gather(values, SHARD, axis=0, tiled=True)]
    dot_general x13 -> x0, matrix products: 56.7 us -> none  [the longest x5 22.1 us: dot_nt(): lax.dot_general(left, right, (((1,), (1,)), ((), ())), preferred_element_...]
    ppermute x0 -> x6, waiting for transfers between devices: none -> 55.3 us  [shift(): lax.ppermute(values, 'z', [(n, (n + step) % size) for n in range(size)])]
    all_to_all x4 -> x3, waiting for transfers between devices: 55 us -> 0.01 us  [exchange_shard(): return lax.all_to_all(values, SHARD, 0, 0, tiled=True)]
    all_gather x1 -> x0, blocking collectives: 47.7 us -> none  [gather_shard(): return lax.all_gather(values, SHARD, axis=0, tiled=True)]
  transfers between devices with their start and end apart: 28 -> 42, of which waited for: 19 -> 14; matrix products, arithmetic and copies ran while one was open for 20% -> 6% of each run, Pallas kernels for 5% -> 24%
where the time goes in v2:
time: 537 us; the launch traced here: 531 us
  waiting for transfers between devices  205 us (38%)
  Pallas kernels  161 us (30%)
  starting transfers between devices  64.2 us (12%)
  blocking collectives  37.9 us (7%)
  local copies, waits for them, and re-layouts  25.6 us (5%)
  other arithmetic  22.9 us (4%)
  between operations  14.7 us (3%)
    pallas_call x14, Pallas kernels, run(): pl.pallas_call(kernel, out_shape=tuple((jax.ShapeDtypeStruct(shape, kind)...  161 us
    ppermute x29, waiting for transfers between devices, swap(): return lax.ppermute(values, axis, [(0, 1), (1, 0)])  150 us
    ppermute x6, waiting for transfers between devices, shift(): lax.ppermute(values, 'z', [(n, (n + step) % size) for n in range(size)])  55.3 us
    all_to_all x1, blocking collectives, exchange_shard(): return lax.all_to_all(values, SHARD, 0, 0, tiled=True)  37.9 us
    ppermute x6, starting transfers between devices, shift(): lax.ppermute(values, 'z', [(n, (n + step) % size) for n in range(size)])  21.1 us
    ppermute x29, starting transfers between devices, swap(): return lax.ppermute(values, axis, [(0, 1), (1, 0)])  20.7 us
    unnamed x87, local copies, waits for them, and re-layouts  19.3 us
    all_to_all x3, starting transfers between devices, exchange_shard(): return lax.all_to_all(values, SHARD, 0, 0, tiled=True)  17.3 us
  transfers between devices with their start and end apart: 42, of which 14 were waited for; matrix products, arithmetic and copies ran while one was open for 6% of the time, Pallas kernels for 24%

profile of v2, /device:TPU:0, one launch (start us, length us, event | category | flops | bytes accessed | tf_op | source)
XLA Modules:
  0.0 531.3 jit_solution(10202857889018054332)
XLA Ops:
  10.5 7.4 %all-to-all-start = ((bf16[8,136,512]{2,1,0:T(8,128)(2,1)}), bf16[8,136,512]{2,1,0:T(8,128)(2,1)S(1)}, u32[]{:S(2)}, u32[]{:S(2)}) async-start(bf16[8,136,512]{2,1,0:T(8,128)(2,1)} %shard_map.179), calls=%async_computation | async-start | bytes 2228224 | tf_op jit(solution)/shard_map/all_to_all | solution.py:710
  31.6 19.5 %collective-permute-done.2.refs_6_ = bf16[256,1152]{1,0:T(8,128)(2,1)S(1)} collective-permute-done((bf16[256,1152]{1,0:T(8,128)(2,1)}, bf16[256,1152]{1,0:T(8,128)(2,1)S(1)}, u32[]{:S(2)}, u32[]{:S(2)}) %collective-permute-start.2) | collective-permute-done | bytes 589856 | tf_op jit(solution)/shard_map/ppermute | solution.py:622
  51.0 14.7 %collective-permute-done.1.refs_2_ = bf16[256,1152]{1,0:T(8,128)(2,1)} collective-permute-done((bf16[256,1152]{1,0:T(8,128)(2,1)}, bf16[256,1152]{1,0:T(8,128)(2,1)}, u32[]{:S(2)}, u32[]{:S(2)}) %collective-permute-start.1) | collective-permute-done | bytes 589856 | tf_op jit(solution)/shard_map/ppermute | solution.py:622
  69.3 6.1 %collective-permute-start.5 = (bf16[256,1152]{1,0:T(8,128)(2,1)}, bf16[256,1152]{1,0:T(8,128)(2,1)}, u32[]{:S(2)}, u32[]{:S(2)}) collective-permute-start(bf16[256,1152]{1,0:T(8,128)(2,1)} %collective-permute-done.1.refs_2_), channel_id=1, source_target_pairs={{0,2},{2,4},{4,6},{6,0},{1,3},{3,5},{5,7},{7,1},{8,10},{10,12},{12... | collective-permute-start | bytes 1769480 | tf_op jit(solution)/shard_map/ppermute | solution.py:622
  76.1 27.9 %collective-permute-done.7.g_b = bf16[256,1152]{1,0:T(8,128)(2,1)S(1)} collective-permute-done((bf16[256,1152]{1,0:T(8,128)(2,1)S(1)}, bf16[256,1152]{1,0:T(8,128)(2,1)S(1)}, u32[]{:S(2)}, u32[]{:S(2)}) %collective-permute-start.7) | collective-permute-done | bytes 589856 | tf_op jit(solution)/shard_map/ppermute | solution.py:607
  110.2 16.9 %collective-permute-done.8.refs_5_ = bf16[256,1152]{1,0:T(8,128)(2,1)S(1)} collective-permute-done((bf16[256,1152]{1,0:T(8,128)(2,1)}, bf16[256,1152]{1,0:T(8,128)(2,1)S(1)}, u32[]{:S(2)}, u32[]{:S(2)}) %collective-permute-start.8) | collective-permute-done | bytes 589856 | tf_op jit(solution)/shard_map/ppermute | solution.py:607
  127.9 38.3 %shard_map.181 = (bf16[2048,512]{1,0:T(8,128)(2,1)}, bf16[8,128,256]{2,1,0:T(8,128)(2,1)}, bf16[8,256,128]{2,1,0:T(8,128)(2,1)}, f32[2048,128]{1,0:T(8,128)}, f3...) custom-call(s32[6]{0:T(128)} %bitcast.73, ...), custom_call_target="tpu_custom_call" | custom-call | flops 30000001024 | bytes 15101476 | tf_op jit(solution)/shard_map/pallas_call | solution.py:595
  166.2 37.9 %all_to_all.20.o_ref = bf16[8,256,128]{2,1,0:T(8,128)(2,1)} all-to-all(bf16[8,256,128]{2,1,0:T(8,128)(2,1)} %get-tuple-element.111), channel_id=1, replica_groups=mesh['dp'=1,'x'=2,'core'=2,'z'=4,'y'=2] {'z','y'}, dimensions={0} | all-to-all | bytes 1048576 | tf_op jit(solution)/shard_map/all_to_all | solution.py:710
  204.1 6.5 %shard_map.182 = (bf16[256,1152]{1,0:T(8,128)(2,1)}, f32[256,1088]{1,0:T(8,128)}, bf16[256,1088]{1,0:T(8,128)(2,1)}, bf16[1088,1088]{1,0:T(8,128)(2,1)}) custom-call(s32[3]{0:T(128)} %pad_add_fusion.spot_ref, bf16[8,256,128]{2,1,0:T(8,128)(2,1)} %all_to_all.20.o_ref, f32[256,128]{1,0:T(8,128)} %get-tuple-element.112.o16_ref, ...), custom_call_target="tpu_custom_call" | custom-call | flops 2000000000 | bytes 10332172 | tf_op jit(solution)/shard_map/pallas_call | solution.py:595
  210.6 14.7 %collective-permute-done.11.h_b = bf16[256,1152]{1,0:T(8,128)(2,1)S(1)} collective-permute-done((bf16[256,1152]{1,0:T(8,128)(2,1)}, bf16[256,1152]{1,0:T(8,128)(2,1)S(1)}, u32[]{:S(2)}, u32[]{:S(2)}) %collective-permute-start.11) | collective-permute-done | bytes 589856 | tf_op jit(solution)/shard_map/ppermute | solution.py:607
  230.6 16.9 %shard_map.183 = (bf16[1024,1088]{1,0:T(8,128)(2,1)}, bf16[1024,1088]{1,0:T(8,128)(2,1)}, f32[256,1152]{1,0:T(8,128)}, f32[256,1152]{1,0:T(8,128)}, bf16[2,256,1152]{2,1,0:T(8,128)(2,1)}, /*index=5*/f32[1,1088]{1,0:T(1,128)}) custom-call(bf16[256,1152]{1,0:T(8,128)(2,1)} %get-tuple-element.114.h_a, bf16[256,1152]{1,0:T(8,128)(2,1)} %copy-done.24, ...), custom_call_target="tpu_custom_call" | custom-call | flops 10000000000 | bytes 17736192 | tf_op jit(solution)/shard_map/pallas_call | solution.py:595
  253.7 16.9 %shard_map.184 = (f32[256,1152]{1,0:T(8,128)}, f32[256,1152]{1,0:T(8,128)}, bf16[2,256,1152]{2,1,0:T(8,128)(2,1)}, bf16[1088,2688]{1,0:T(8,128)(2,1)}) custom-call(bf16[256,1152]{1,0:T(8,128)(2,1)} %get-tuple-element.114.h_a, bf16[256,1152]{1,0:T(8,128)(2,1)} %copy-done.24, bf16[2,256,1152]{2,1,0:T(8,128)(2,1)} %copy-done.34, bf16[256,1152]{1,0:T(8,128)(2,1)} %copy-done.6, ...), custom_call_target="tpu_custom_call" | custom-call | flops 10000000000 | bytes 23576576 | tf_op jit(solution)/shard_map/pallas_call | solution.py:595
  272.3 9.7 %shard_map.185 = (f32[256,1088]{1,0:T(8,128)}, bf16[8,256,128]{2,1,0:T(8,128)(2,1)}, bf16[256,128]{1,0:T(8,128)(2,1)}, f32[1088,384]{1,0:T(8,128)}, f32[1088,384...) custom-call(s32[3]{0:T(128)} %pad_add_fusion.spot_ref, f32[256,1152]{1,0:T(8,128)} %get-tuple-element.136.kept_ref, ...), custom_call_target="tpu_custom_call" | custom-call | flops 3000000000 | bytes 13731340 | tf_op jit(solution)/shard_map/pallas_call | solution.py:595
  288.7 20.0 %collective-permute-done.18.c_ref = bf16[1088,384]{1,0:T(8,128)(2,1)S(1)} collective-permute-done((bf16[1088,384]{1,0:T(8,128)(2,1)S(1)}, bf16[1088,384]{1,0:T(8,128)(2,1)S(1)}, u32[]{:S(2)}, u32[]{:S(2)}) %collective-permute-start.18) | collective-permute-done | bytes 835616 | tf_op jit(solution)/shard_map/ppermute | solution.py:607
  315.3 38.9 %shard_map.187 = (bf16[2048,512]{1,0:T(8,128)(2,1)}, bf16[256,128]{1,0:T(8,128)(2,1)}, bf16[256,1152]{1,0:T(8,128)(2,1)}, bf16[256,1152]{1,0:T(8,128)(2,1)}, bf1...) custom-call(s32[6]{0:T(128)} %bitcast.74, ...), custom_call_target="tpu_custom_call" | custom-call | flops 30000001024 | bytes 12847128 | tf_op jit(solution)/shard_map/pallas_call | solution.py:595
  356.2 8.5 %shard_map.188 = (f32[1088,256]{1,0:T(8,128)}, f32[1088,256]{1,0:T(8,128)}, bf16[2,1088,256]{2,1,0:T(8,128)(2,1)}) custom-call(s32[3]{0:T(128)} %pad_add_fusion.spot_ref, bf16[256,1152]{1,0:T(8,128)(2,1)} %shard_map.178.refs_0_, bf16[256,1152]{1,0:T(8,128)(2,1)} %collective-permute-done.refs_1_, bf16[256,1152]{1,0:T(8,128)(2,1)} %collective-permute-done.1.refs_2_, ...), custom_call_target="tpu_custom_call" | custom-call | flops 3000000000 | bytes 10223628 | tf_op jit(solution)/shard_map/pallas_call | solution.py:595
  372.6 5.1 collective-permute-start.22
  377.7 14.3 %collective-permute-done.24 = bf16[256,1152]{1,0:T(8,128)(2,1)} collective-permute-done((bf16[256,1152]{1,0:T(8,128)(2,1)}, bf16[256,1152]{1,0:T(8,128)(2,1)}, u32[]{:S(2)}, u32[]{:S(2)}) %collective-permute-start.24) | collective-permute-done | bytes 589856 | tf_op jit(solution)/shard_map/ppermute | solution.py:607
  398.2 28.9 %collective-permute-done.20 = bf16[256,1152]{1,0:T(8,128)(2,1)S(1)} collective-permute-done((bf16[256,1152]{1,0:T(8,128)(2,1)}, bf16[256,1152]{1,0:T(8,128)(2,1)S(1)}, u32[]{:S(2)}, u32[]{:S(2)}) %collective-permute-start.20) | collective-permute-done | bytes 589856 | tf_op jit(solution)/shard_map/ppermute | solution.py:607
  432.4 21.1 %collective-permute-done.23.a_ref = bf16[256,1152]{1,0:T(8,128)(2,1)S(1)} collective-permute-done((bf16[256,1152]{1,0:T(8,128)(2,1)}, bf16[256,1152]{1,0:T(8,128)(2,1)S(1)}, u32[]{:S(2)}, u32[]{:S(2)}) %collective-permute-start.23) | collective-permute-done | bytes 589856 | tf_op jit(solution)/shard_map/ppermute | solution.py:622
  463.9 5.6 %all-to-all-start.3 = ((bf16[8,136,256]{2,1,0:T(8,128)(2,1)}), bf16[8,136,256]{2,1,0:T(8,128)(2,1)S(1)}, u32[]{:S(2)}, u32[]{:S(2)}) async-start(bf16[8,136,256]{2,1,0:T(8,128)(2,1)} %bitcast.24), calls=%async_computation.3 | async-start | bytes 1114112 | tf_op jit(solution)/shard_map/all_to_all | solution.py:710
  470.4 9.6 %collective-permute-done.33 = f32[12,1088]{1,0:T(8,128)S(1)} collective-permute-done((f32[12,1088]{1,0:T(8,128)S(1)}, f32[12,1088]{1,0:T(8,128)S(1)}, u32[]{:S(2)}, u32[]{:S(2)}) %collective-permute-start.33) | collective-permute-done | bytes 52256 | tf_op jit(solution)/shard_map/ppermute | solution.py:607
  498.1 7.0 %collective-permute-done.28.b_ref = bf16[136,1152]{1,0:T(8,128)(2,1)S(1)} collective-permute-done((bf16[136,1152]{1,0:T(8,128)(2,1)}, bf16[136,1152]{1,0:T(8,128)(2,1)S(1)}, u32[]{:S(2)}, u32[]{:S(2)}) %collective-permute-start.28) | collective-permute-done | bytes 313376 | tf_op jit(solution)/shard_map/ppermute | solution.py:607
  517.9 6.4 %shard_map.192 = (f32[136,4352]{1,0:T(8,128)}, f32[544,1088]{1,0:T(8,128)}, f32[136,1088]{1,0:T(8,128)}) custom-call(s32[3]{0:T(128)} %pad_add_fusion.spot_ref, bf16[136,2688]{1,0:T(8,128)(2,1)} %reduce-scatter.4.cloned.1.call-done.a_ref, bf16[136,2688]{1,0:T(8,128)(2,1)} %copy-done.4, bf16[2,136,2688]{2,1,0:T(8,128)(2,1)} %copy-done.9), custom_call_target="tpu_custom_call" | custom-call | bytes 8251404 | tf_op jit(solution)/shard_map/pallas_call | solution.py:595
  (212 shorter events, 117.8 us)
Async XLA Ops:
  10.5 55.2 %all-to-all-start = ((bf16[8,136,512]{2,1,0:T(8,128)(2,1)}), bf16[8,136,512]{2,1,0:T(8,128)(2,1)S(1)}, u32[]{:S(2)}, u32[]{:S(2)}) async-start(bf16[8,136,512]{2,1,0:T(8,128)(2,1)} %shard_map.179), calls=%async_computation | async-start | bytes 2228224 | tf_op jit(solution)/shard_map/all_to_all | solution.py:710
  18.0 211.7 %all-gather.2.cloned.1.call-start = ((), (), s32[]{:S(2)}) async-start(), calls=%async_computation.5 | async-start | bytes 5640192 | tf_op jit(solution)/shard_map/all_gather | solution.py:702
  22.4 28.6 %collective-permute-start.2 = (bf16[256,1152]{1,0:T(8,128)(2,1)}, bf16[256,1152]{1,0:T(8,128)(2,1)S(1)}, u32[]{:S(2)}, u32[]{:S(2)}) collective-permute-start(bf16[256,1152]{1,0:T(8,128)(2,1)} %shard_map.178.refs_0_), channel_id=1, source_target_pairs={{0,6},{2,0},{4,2},{6,4},{1,7},{3,1},{5,3},{7,5},{8,14},{10,8},{12,... | collective-permute-start | bytes 1769480 | tf_op jit(solution)/shard_map/ppermute | solution.py:622
  26.2 39.6 %collective-permute-start.1 = (bf16[256,1152]{1,0:T(8,128)(2,1)}, bf16[256,1152]{1,0:T(8,128)(2,1)}, u32[]{:S(2)}, u32[]{:S(2)}) collective-permute-start(bf16[256,1152]{1,0:T(8,128)(2,1)} %shard_map.178.refs_0_), channel_id=1, source_target_pairs={{0,2},{2,4},{4,6},{6,0},{1,3},{3,5},{5,7},{7,1},{8,10},{10,12},{12... | collective-permute-start | bytes 1769480 | tf_op jit(solution)/shard_map/ppermute | solution.py:622
  26.2 39.6 %collective-permute-start = (bf16[256,1152]{1,0:T(8,128)(2,1)}, bf16[256,1152]{1,0:T(8,128)(2,1)}, u32[]{:S(2)}, u32[]{:S(2)}) collective-permute-start(bf16[256,1152]{1,0:T(8,128)(2,1)} %shard_map.178.refs_0_), channel_id=1, source_target_pairs={{0,1},{1,0},{2,3},{3,2},{4,5},{5,4},{6,7},{7,6},{8,9},{9,8},{10,11... | collective-permute-start | bytes 1769480 | tf_op jit(solution)/shard_map/ppermute | solution.py:607
  65.8 39.9 %collective-permute-start.6 = (bf16[1088,512]{1,0:T(8,128)(2,1)S(1)}, bf16[1088,512]{1,0:T(8,128)(2,1)S(1)}, u32[]{:S(2)}, u32[]{:S(2)}) collective-permute-start(bf16[1088,512]{1,0:T(8,128)(2,1)S(1)} %bitcast.56), channel_id=1, source_target_pairs={{0,16},{16,0},{1,17},{17,1},{2,18},{18,2},{3,19},{19,3},{4,20},{20... | collective-permute-start | bytes 3342344 | tf_op jit(solution)/shard_map/ppermute | solution.py:607
  67.6 36.4 %collective-permute-start.7 = (bf16[256,1152]{1,0:T(8,128)(2,1)S(1)}, bf16[256,1152]{1,0:T(8,128)(2,1)S(1)}, u32[]{:S(2)}, u32[]{:S(2)}) collective-permute-start(bf16[256,1152]{1,0:T(8,128)(2,1)S(1)} %pad.15.g_a.cot_ref), channel_id=1, source_target_pairs={{0,16},{16,0},{1,17},{17,1},{2,18},{18,2},{3,19},{19,3},{4,20},{20... | collective-permute-start | bytes 1769480 | tf_op jit(solution)/shard_map/ppermute | solution.py:607
  67.9 36.1 %collective-permute-start.4 = (bf16[256,1152]{1,0:T(8,128)(2,1)}, bf16[256,1152]{1,0:T(8,128)(2,1)S(1)}, u32[]{:S(2)}, u32[]{:S(2)}) collective-permute-start(bf16[256,1152]{1,0:T(8,128)(2,1)} %copy-done.35), channel_id=1, source_target_pairs={{0,1},{1,0},{2,3},{3,2},{4,5},{5,4},{6,7},{7,6},{8,9},{9,8},{10,11... | collective-permute-start | bytes 1769480 | tf_op jit(solution)/shard_map/ppermute | solution.py:607
  69.3 34.7 %collective-permute-start.5 = (bf16[256,1152]{1,0:T(8,128)(2,1)}, bf16[256,1152]{1,0:T(8,128)(2,1)}, u32[]{:S(2)}, u32[]{:S(2)}) collective-permute-start(bf16[256,1152]{1,0:T(8,128)(2,1)} %collective-permute-done.1.refs_2_), channel_id=1, source_target_pairs={{0,2},{2,4},{4,6},{6,0},{1,3},{3,5},{5,7},{7,1},{8,10},{10,12},{12... | collective-permute-start | bytes 1769480 | tf_op jit(solution)/shard_map/ppermute | solution.py:622
  75.4 29.4 %collective-permute-start.3 = (bf16[256,1152]{1,0:T(8,128)(2,1)}, bf16[256,1152]{1,0:T(8,128)(2,1)S(1)}, u32[]{:S(2)}, u32[]{:S(2)}) collective-permute-start(bf16[256,1152]{1,0:T(8,128)(2,1)} %collective-permute-done.1.refs_2_), channel_id=1, source_target_pairs={{0,1},{1,0},{2,3},{3,2},{4,5},{5,4},{6,7},{7,6},{8,9},{9,8},{10,11... | collective-permute-start | bytes 1769480 | tf_op jit(solution)/shard_map/ppermute | solution.py:607
  282.0 32.5 %all-to-all-start.2 = ((bf16[8,256,128]{2,1,0:T(8,128)(2,1)}), bf16[8,256,128]{2,1,0:T(8,128)(2,1)S(1)}, u32[]{:S(2)}, u32[]{:S(2)}) async-start(bf16[8,256,128]{2,1,0:T(8,128)(2,1)} %get-tuple-element.142), calls=%async_computation.2 | async-start | bytes 1048576 | tf_op jit(solution)/shard_map/all_to_all | solution.py:710
  286.3 167.2 %reduce-scatter.4.cloned.1.call-start = ((), (), s32[]{:S(2)}) async-start(), calls=%async_computation.6 | async-start | bytes 6580224
  355.8 36.2 %collective-permute-start.24 = (bf16[256,1152]{1,0:T(8,128)(2,1)}, bf16[256,1152]{1,0:T(8,128)(2,1)}, u32[]{:S(2)}, u32[]{:S(2)}) collective-permute-start(bf16[256,1152]{1,0:T(8,128)(2,1)} %get-tuple-element.158), channel_id=1, source_target_pairs={{0,1},{1,0},{2,3},{3,2},{4,5},{5,4},{6,7},{7,6},{8,9},{9,8},{10,11... | collective-permute-start | bytes 1769480 | tf_op jit(solution)/shard_map/ppermute | solution.py:607
  364.8 32.4 %collective-permute-start.26 = (bf16[2,1088,256]{2,1,0:T(8,128)(2,1)}, bf16[2,1088,256]{2,1,0:T(8,128)(2,1)S(1)}, u32[]{:S(2)}, u32[]{:S(2)}) collective-permute-start(bf16[2,1088,256]{2,1,0:T(8,128)(2,1)} %get-tuple-element.161), channel_id=1, source_target_pairs={{0,8},{8,0},{1,9},{9,1},{2,10},{10,2},{3,11},{11,3},{4,12},{12,4},... | collective-permute-start | bytes 3342344 | tf_op jit(solution)/shard_map/ppermute | solution.py:607
  364.8 67.5 %collective-permute-start.19 = (bf16[256,1152]{1,0:T(8,128)(2,1)}, bf16[256,1152]{1,0:T(8,128)(2,1)S(1)}, u32[]{:S(2)}, u32[]{:S(2)}) collective-permute-start(bf16[256,1152]{1,0:T(8,128)(2,1)} %get-tuple-element.152), channel_id=1, source_target_pairs={{0,1},{1,0},{2,3},{3,2},{4,5},{5,4},{6,7},{7,6},{8,9},{9,8},{10,11... | collective-permute-start | bytes 1769480 | tf_op jit(solution)/shard_map/ppermute | solution.py:607
  366.5 60.6 %collective-permute-start.20 = (bf16[256,1152]{1,0:T(8,128)(2,1)}, bf16[256,1152]{1,0:T(8,128)(2,1)S(1)}, u32[]{:S(2)}, u32[]{:S(2)}) collective-permute-start(bf16[256,1152]{1,0:T(8,128)(2,1)} %get-tuple-element.154), channel_id=1, source_target_pairs={{0,1},{1,0},{2,3},{3,2},{4,5},{5,4},{6,7},{7,6},{8,9},{9,8},{10,11... | collective-permute-start | bytes 1769480 | tf_op jit(solution)/shard_map/ppermute | solution.py:607
  372.6 54.5 %collective-permute-start.22 = (bf16[256,1152]{1,0:T(8,128)(2,1)S(1)}, bf16[256,1152]{1,0:T(8,128)(2,1)S(1)}, u32[]{:S(2)}, u32[]{:S(2)}) collective-permute-start(bf16[256,1152]{1,0:T(8,128)(2,1)S(1)} %add_convert_fusion.2), channel_id=1, source_target_pairs={{0,6},{2,0},{4,2},{6,4},{1,7},{3,1},{5,3},{7,5},{8,14},{10,8},{12,... | collective-permute-start | bytes 1769480 | tf_op jit(solution)/shard_map/ppermute | solution.py:622
  394.1 38.2 %collective-permute-start.25 = (bf16[256,1152]{1,0:T(8,128)(2,1)}, bf16[256,1152]{1,0:T(8,128)(2,1)S(1)}, u32[]{:S(2)}, u32[]{:S(2)}) collective-permute-start(bf16[256,1152]{1,0:T(8,128)(2,1)} %add_convert_fusion), channel_id=1, source_target_pairs={{0,2},{2,4},{4,6},{6,0},{1,3},{3,5},{5,7},{7,1},{8,10},{10,12},{12... | collective-permute-start | bytes 1769480 | tf_op jit(solution)/shard_map/ppermute | solution.py:622
  398.2 34.2 %collective-permute-start.27 = (bf16[1088,256]{1,0:T(8,128)(2,1)}, bf16[1088,256]{1,0:T(8,128)(2,1)}, u32[]{:S(2)}, u32[]{:S(2)}) collective-permute-start(bf16[1088,256]{1,0:T(8,128)(2,1)} %fusion.9), channel_id=1, source_target_pairs={{0,16},{16,0},{1,17},{17,1},{2,18},{18,2},{3,19},{19,3},{4,20},{20... | collective-permute-start | bytes 1671176 | tf_op jit(solution)/shard_map/ppermute | solution.py:607
  428.2 25.3 %collective-permute-start.23 = (bf16[256,1152]{1,0:T(8,128)(2,1)}, bf16[256,1152]{1,0:T(8,128)(2,1)S(1)}, u32[]{:S(2)}, u32[]{:S(2)}) collective-permute-start(bf16[256,1152]{1,0:T(8,128)(2,1)} %add_convert_fusion.1), channel_id=1, source_target_pairs={{0,6},{2,0},{4,2},{6,4},{1,7},{3,1},{5,3},{7,5},{8,14},{10,8},{12,... | collective-permute-start | bytes 1769480 | tf_op jit(solution)/shard_map/ppermute | solution.py:622
  431.3 50.3 %collective-permute-start.14 = (bf16[2,256,1152]{2,1,0:T(8,128)(2,1)}, bf16[2,256,1152]{2,1,0:T(8,128)(2,1)}, u32[]{:S(2)}, u32[]{:S(2)}) collective-permute-start(bf16[2,256,1152]{2,1,0:T(8,128)(2,1)} %get-tuple-element.127), channel_id=1, source_target_pairs={{0,8},{8,0},{1,9},{9,1},{2,10},{10,2},{3,11},{11,3},{4,12},{12,4},... | collective-permute-start | bytes 3538952 | tf_op jit(solution)/shard_map/ppermute | solution.py:607
  459.6 27.8 %collective-permute-start.30 = (bf16[136,2688]{1,0:T(8,128)(2,1)S(1)}, bf16[136,2688]{1,0:T(8,128)(2,1)S(1)}, u32[]{:S(2)}, u32[]{:S(2)}) collective-permute-start(bf16[136,2688]{1,0:T(8,128)(2,1)S(1)} %copy-done.3), channel_id=1, source_target_pairs={{0,16},{16,0},{1,17},{17,1},{2,18},{18,2},{3,19},{19,3},{4,20},{20... | collective-permute-start | bytes 2193416 | tf_op jit(solution)/shard_map/ppermute | solution.py:607
  463.9 24.9 %all-to-all-start.3 = ((bf16[8,136,256]{2,1,0:T(8,128)(2,1)}), bf16[8,136,256]{2,1,0:T(8,128)(2,1)S(1)}, u32[]{:S(2)}, u32[]{:S(2)}) async-start(bf16[8,136,256]{2,1,0:T(8,128)(2,1)} %bitcast.24), calls=%async_computation.3 | async-start | bytes 1114112 | tf_op jit(solution)/shard_map/all_to_all | solution.py:710
  488.8 27.9 %collective-permute-start.31 = (bf16[2,136,2688]{2,1,0:T(8,128)(2,1)}, bf16[2,136,2688]{2,1,0:T(8,128)(2,1)S(1)}, u32[]{:S(2)}, u32[]{:S(2)}) collective-permute-start(bf16[2,136,2688]{2,1,0:T(8,128)(2,1)} %pad_maximum_fusion.1), channel_id=1, source_target_pairs={{0,8},{8,0},{1,9},{9,1},{2,10},{10,2},{3,11},{11,3},{4,12},{12,4},... | collective-permute-start | bytes 4386824 | tf_op jit(solution)/shard_map/ppermute | solution.py:607
  (59 other events, 713.8 us)
Sparse Core Ops, SparseCore 0:
  105.9 100.0 all-gather.1
  314.7 136.7 reduce-scatter.3
